TPU v7x, 128 devices: a whole 4x4x4 slice. The times are simulated.
128 devices in a mesh: stn: 16 (over y, z), blk: 8 (over x, core).
Axes of the slice: x: 4, y: 4, z: 4, core: 2. Of those that a mesh axis runs over, the one named last changes fastest.
Arguments:
- voltages: bfloat16 [2, 512, 524288], P(None, 'stn', 'blk'), may hold values from -12 to 12
- taps: float32 [16, 4096], replicated, may hold values from -1.5 to 1.5
- model_phase: float32 [512], replicated, may hold values from -3.140625 to 3.140625
Outputs:
- gains: float32 [2, 4096, 512], P(None, ('stn', 'blk'))
All inputs are finite; a program needn't handle non-finite values.
Results may differ from a plain program's by a relative error of at most 0.0041.
Values may be sent and summed in bfloat16 or wider, within the bound.
A program may use at most 192 MiB of HBM per device.

v0:
```python
import jax
import jax.numpy as jnp
from jax import lax
from jax.sharding import PartitionSpec as P

ITERS = 4


epsilon = 1e-06


def shifted(block, axis, distance):
    devices = range(lax.axis_size(axis))
    route = [(i - distance, i) for i in devices if i - distance in devices]
    return lax.ppermute(block, axis, route)


def tables(size_one, size_two, total):
    first = jnp.arange(size_one, dtype=jnp.int32)
    second = jnp.arange(size_two, dtype=jnp.int32)
    return first[:, None] * second[None, :] % total


def transform(filtered):
    channels = filtered.shape[-1]
    bits = channels.bit_length() - 1
    radix_one = 2 ** (bits // 2)
    radix_two = channels // radix_one
    lead = filtered.shape[:3]
    wave = filtered.reshape(lead + (radix_one, radix_two))
    highest = lax.Precision.HIGHEST
    angle_one = (
        -2.0 * jnp.pi * tables(radix_one, radix_one, radix_one).astype(jnp.float32) / radix_one
    )
    cos_one = jnp.cos(angle_one)
    sin_one = jnp.sin(angle_one)
    matrix_one = jnp.stack(
        [jnp.stack([cos_one, -sin_one], axis=1), jnp.stack([sin_one, cos_one], axis=1)]
    )
    section = jnp.einsum("qkpa,pisan->qiskn", matrix_one, wave, precision=highest)
    angle_tw = -2.0 * jnp.pi * tables(radix_one, radix_two, channels).astype(jnp.float32) / channels
    twist_re = jnp.cos(angle_tw)
    twist_im = jnp.sin(angle_tw)
    turned = jnp.stack(
        [
            section[0] * twist_re - section[1] * twist_im,
            section[0] * twist_im + section[1] * twist_re,
        ]
    )
    angle_two = (
        -2.0 * jnp.pi * tables(radix_two, radix_two, radix_two).astype(jnp.float32) / radix_two
    )
    cos_two = jnp.cos(angle_two)
    sin_two = jnp.sin(angle_two)
    matrix_two = jnp.stack(
        [jnp.stack([cos_two, sin_two], axis=1), jnp.stack([-sin_two, cos_two], axis=1)]
    )
    final = jnp.einsum("piskn,pnqb->qisbk", turned, matrix_two, precision=highest)
    return final.reshape(lead + (channels,))


def calibrate(block, model_re, model_im):
    count = block.shape[2]
    highest = lax.Precision.HIGHEST
    floated = block.astype(jnp.float32)
    self_power = jnp.sum(floated * floated, axis=(1, 3))
    gain_re = jnp.ones((block.shape[0], count), jnp.float32)
    gain_im = jnp.zeros((block.shape[0], count), jnp.float32)
    for iteration in range(1, ITERS + 1):
        weight_re = gain_re * model_re - gain_im * model_im
        weight_im = gain_re * model_im + gain_im * model_re
        vectors = jnp.stack([weight_re, weight_im], axis=1)
        down = jnp.einsum("cpjt,cqj->cpqt", floated, vectors, precision=highest)
        back_re = down[:, 0, 0] + down[:, 1, 1]
        back_im = down[:, 0, 1] - down[:, 1, 0]
        backs = jnp.stack([back_re, back_im], axis=1)
        upward = jnp.einsum("cpit,cqt->cpqi", floated, backs, precision=highest)
        out_re = upward[:, 0, 0] - upward[:, 1, 1]
        out_im = upward[:, 0, 1] + upward[:, 1, 0]
        prod_re = out_re - self_power * weight_re
        prod_im = out_im - self_power * weight_im
        numer_re = model_re * prod_re + model_im * prod_im
        numer_im = model_re * prod_im - model_im * prod_re
        own_power = weight_re * weight_re + weight_im * weight_im
        denom = jnp.sum(own_power, axis=1, keepdims=True) - own_power + epsilon
        new_re = numer_re / denom
        new_im = numer_im / denom
        if iteration % 2 == 0:
            gain_re = (new_re + gain_re) * 0.5
            gain_im = (new_im + gain_im) * 0.5
        else:
            gain_re = new_re
            gain_im = new_im
    return jnp.stack([gain_re, gain_im], axis=1)


def on_device(voltages, taps, model_phase):
    local_inputs = voltages.shape[1]
    tap_count = taps.shape[0]
    channels = taps.shape[1]
    spectra_here = voltages.shape[2] // channels
    tail = voltages[:, :, (spectra_here - tap_count + 1) * channels :]
    earlier = shifted(tail, "blk", 1)
    extended = jnp.concatenate([earlier, voltages], axis=2).reshape(
        2, local_inputs, spectra_here + tap_count - 1, channels
    )
    filtered = jnp.zeros((2, local_inputs, spectra_here, channels), jnp.float32)
    for tap_index in range(tap_count):
        filtered = filtered + taps[tap_index] * extended[
            :, :, tap_index : tap_index + spectra_here, :
        ].astype(jnp.float32)
    spectrum = transform(filtered)
    local_power = jnp.sum(spectrum * spectrum, axis=(0, 2, 3))
    total_power = lax.psum(local_power, "blk")
    stations_axis = lax.axis_size("stn")
    blocks_axis = lax.axis_size("blk")
    scale = 1.0 / jnp.sqrt(total_power / (spectra_here * blocks_axis * channels) + epsilon)
    quantized = (spectrum * scale[None, :, None, None]).astype(jnp.bfloat16)
    owned = channels // (stations_axis * blocks_axis)
    moved = lax.all_to_all(
        quantized.reshape(2, 1, local_inputs, spectra_here, channels),
        ("stn", "blk"),
        split_axis=4,
        concat_axis=1,
        tiled=True,
    )
    turned = moved.reshape(
        2, stations_axis, blocks_axis, local_inputs, spectra_here, owned
    ).transpose(0, 1, 3, 2, 4, 5)
    all_inputs = stations_axis * local_inputs
    all_spectra = blocks_axis * spectra_here
    by_channel = turned.transpose(5, 0, 1, 2, 3, 4).reshape(owned, 2, all_inputs, all_spectra)
    block_size = min(8, owned)
    blocks = by_channel.reshape(owned // block_size, block_size, 2, all_inputs, all_spectra)
    model_re = jnp.cos(model_phase)
    model_im = jnp.sin(model_phase)
    solved = lax.map(lambda block: calibrate(block, model_re, model_im), blocks)
    return solved.reshape(owned, 2, all_inputs).transpose(1, 0, 2)


def solution(mesh):
    in_specs = (P(None, "stn", "blk"), P(), P())
    out_specs = P(None, ("stn", "blk"), None)
    return jax.shard_map(
        on_device, mesh=mesh, in_specs=in_specs, out_specs=out_specs, check_vma=False
    )
```

profile of v0, /device:TPU:1, one launch (start us, length us, event | category | flops | bytes accessed | tf_op | source)
XLA Modules:
  0.0 828.3 jit_solution(6951065532734453294)
XLA Ops:
  0.0 7.4 slice.204
  7.4 4.5 collective-permute-start
  12.4 2.3 fusion.86
  14.7 82.3 %collective-permute-done = bf16[2,32,61440]{2,1,0:T(8,128)(2,1)S(1)} collective-permute-done((bf16[2,32,61440]{2,1,0:T(8,128)(2,1)}, bf16[2,32,61440]{2,1,0:T(8,128)(2,1)S(1)}, u32[]{:S(2)}, u32[]{:S(2)}) %collective-permute-start) | collective-permute-done | bytes 7864352 | tf_op jit(solution)/shard_map/ppermute | solution.py:15
  97.0 6.4 pad_maximum_fusion
  103.4 17.4 %reshape.3932 = bf16[2,32,31,4096]{3,2,1,0:T(8,128)(2,1)} reshape(bf16[2,32,126976]{2,1,0:T(8,128)(2,1)} %pad_maximum_fusion) | data formatting | bytes 32505856 | tf_op jit(solution)/shard_map/reshape | solution.py:104
  120.8 76.6 %multiply_add_fusion.10 = f32[2,32,16,4096]{3,2,1,0:T(8,128)} fusion(bf16[2,32,31,4096]{3,2,1,0:T(8,128)(2,1)} %reshape.3932, f32[4096]{0:T(1024)S(1)} %bitcast.413, f32[4096]{0:T(1024)S(1)} %bitcast.414, f32[4096]{0:T(1024)S(1)} %bitcast.400, f32[4096]{0:T(1024)S(1)} %bitcast.401, f32[4096]{0:T(1024)S(1)} %bitcast.402, f32[4096]{0:T(1024)S(1)} %bitcast.403, ...), kind=kLoop, calls=%fused_computation.133 | loop fusion | flops 197132288 | bytes 151257088 | tf_op jit(solution)/shard_map/add | solution.py:109
  197.4 27.1 %reshape.3933 = f32[2,32,16,64,64]{4,3,2,1,0:T(8,128)} reshape(f32[2,32,16,4096]{3,2,1,0:T(8,128)} %multiply_add_fusion.10) | data formatting | bytes 33554432 | tf_op jit(solution)/shard_map/reshape | solution.py:30
  224.5 58.3 %fusion.51 = f32[2,32,16,64,64]{3,4,0,2,1:T(8,128)} fusion(f32[2,32,16,64,64]{4,3,2,1,0:T(8,128)} %reshape.3933, f32[2,64,2,64,1,1]{3,1,2,0,5,4:T(8,128)S(1)} %maximum_bitcast_fusion.21), kind=kOutput, calls=%fused_computation.135 | convolution fusion | flops 6442450944 | bytes 33619968 | tf_op jit(solution)/shard_map/qkpa,pisan->qiskn/dot_general | solution.py:40
  282.8 22.0 %multiply_subtract_fusion.6 = (f32[1,32,16,64,64]{3,4,0,2,1:T(8,128)}, f32[1,32,16,64,64]{3,4,0,2,1:T(8,128)}) fusion(f32[2,32,16,64,64]{3,4,0,2,1:T(8,128)} %fusion.51, f32[64,64]{0,1:T(8,128)S(1)} %get-tuple-element.132, f32[64,64]{0,1:T(8,128)S(1)} %get-tuple-element.133), kind=kLoop, calls=%fused_computation.132 | loop fusion | flops 12582912 | bytes 33587200 | tf_op jit(solution)/shard_map/sub | solution.py:46
  304.8 40.3 %multiply_reduce_fusion.1 = (f32[32]{0:T(128)S(1)}, f32[2,32,16,64,64]{4,3,2,1,0:T(8,128)}) fusion(f32[1,32,16,64,64]{3,4,0,2,1:T(8,128)} %get-tuple-element.103, f32[1,32,16,64,64]{3,4,0,2,1:T(8,128)} %get-tuple-element.102, f32[1,64,2,64]{3,1,2,0:T(8,128)S(1)} %get-tuple-element.125, f32[1,64,2,64]{3,1,2,0:T(8,128)S(1)} %get-tuple-element.120), kind=kOutput, calls=%fused_computation.128 | convolution fusion | flops 6455050240 | bytes 33620096 | tf_op jit(solution)/shard_map/piskn,pnqb->qisbk/dot_general | solution.py:58
  345.1 27.9 %reshape.3934 = f32[2,1,32,16,4096]{4,3,2,1,0:T(8,128)} reshape(f32[2,32,16,64,64]{4,3,2,1,0:T(8,128)} %get-tuple-element.129) | data formatting | bytes 33554432 | tf_op jit(solution)/shard_map/reshape | solution.py:59
  373.0 13.1 %psum.7 = f32[32]{0:T(128)S(1)} all-reduce(f32[32]{0:T(128)S(1)} %get-tuple-element.128), channel_id=1, replica_groups=mesh['stn'=16,'blk'=8] {'blk'}, use_global_device_ids=true, to_apply=%region_1.2 | all-reduce | flops 32 | bytes 256 | tf_op jit(solution)/shard_map/psum | solution.py:114
  386.1 9.2 %multiply_convert_fusion = bf16[2,1,32,16,4096]{4,3,2,1,0:T(8,128)(2,1)} fusion(f32[2,1,32,16,4096]{4,3,2,1,0:T(8,128)} %reshape.3934, f32[32]{0:T(128)S(1)} %add_rsqrt_fusion), kind=kLoop, calls=%fused_computation.130 | loop fusion | flops 8388608 | bytes 25165952 | tf_op jit(solution)/shard_map/convert_element_type | solution.py:118
  395.3 54.8 %copy.175 = bf16[2,1,32,16,4096]{2,3,1,0,4:T(8,128)(2,1)} copy(bf16[2,1,32,16,4096]{4,3,2,1,0:T(8,128)(2,1)} %multiply_convert_fusion) | data formatting | bytes 16777216 | tf_op jit(solution)/shard_map/convert_element_type | solution.py:118
  450.1 48.5 %reshape.3951 = bf16[128,2,16384]{2,1,0:T(2,128)(2,1)} reshape(bf16[4096,2,1,16,32]{4,3,2,1,0:T(8,128)(2,1)} %bitcast.378) | data formatting | bytes 16777216
  498.6 9.0 %all-to-all-start = ((bf16[128,2,16384]{2,1,0:T(2,128)(2,1)}), bf16[128,2,16384]{2,1,0:T(2,128)(2,1)}, u32[]{:S(2)}, u32[]{:S(2)}) async-start(bf16[128,2,16384]{2,1,0:T(2,128)(2,1)} %reshape.3951), calls=%async_computation | async-start | bytes 16777216 | tf_op jit(solution)/shard_map/all_to_all | solution.py:120
  507.7 100.6 %all-to-all-done = bf16[128,2,16384]{2,1,0:T(2,128)(2,1)} async-done(((bf16[128,2,16384]{2,1,0:T(2,128)(2,1)}), bf16[128,2,16384]{2,1,0:T(2,128)(2,1)}, u32[]{:S(2)}, u32[]{:S(2)}) %all-to-all-start) | async-done | bytes 8388640 | tf_op jit(solution)/shard_map/all_to_all | solution.py:120
  608.2 42.5 %reshape.3952 = bf16[4096,2,1,16,32]{4,3,2,1,0:T(8,128)(2,1)} reshape(bf16[128,2,16384]{2,1,0:T(2,128)(2,1)} %all-to-all-done) | data formatting | bytes 16777216
  650.8 53.9 %copy.178 = bf16[32,2,16,32,8,16]{3,2,5,4,1,0:T(8,128)(2,1)} copy(bf16[32,2,16,32,8,16]{3,5,1,0,4,2:T(8,128)(2,1)} %bitcast.379) | data formatting | bytes 16777216 | tf_op jit(solution)/shard_map/transpose;transpose | solution.py:132
  704.7 43.7 %reshape_reshape.3 = bf16[4,8,2,512,128]{3,4,2,1,0:T(8,128)(2,1)} reshape(bf16[32,2,16,32,8,16]{3,2,5,4,1,0:T(8,128)(2,1)} %copy.178) | data formatting | bytes 16777216 | tf_op jit(solution)/shard_map/reshape;reshape | solution.py:134
  748.4 78.8 %while.10 = (s32[]{:T(128)}, f32[4,8,2,512]{3,1,0,2:T(8,128)S(1)}, f32[512]{0:T(512)S(1)}, f32[512]{0:T(512)S(1)}, bf16[4,8,2,512,128]{3,4,2,1,0:T(8,128)(2,1)}, /*index=5*/s32[]{:T(128)}) while((s32[]{:T(128)}, f32[4,8,2,512]{3,1,0,2:T(8,128)S(1)}, f32[512]{0:T(512)S(1)}, f32[512]{0:T(512)S(1)}, bf16[4,8,2,512,128]{3,4,2,1,0:T(8,128)(2,1)}, ...), condition=%wide.region_8.9_spmd, body=%wide.region_2.8_spmd.sunk | while | flops 205393376 | bytes 30404980 | solution.py:137
  749.3 1.8 constant_dynamic-slice_fusion.2
  751.1 1.7 fusion.146
  753.8 2.4 copy.287
  756.2 2.2 multiply_reduce_fusion.3
  759.1 1.7 fusion.151
  762.1 1.7 fusion.155
  765.2 1.7 fusion.158
  768.9 1.8 constant_dynamic-slice_fusion.2
  770.7 1.7 fusion.146
  773.5 2.4 copy.287
  775.9 2.2 multiply_reduce_fusion.3
  778.7 1.7 fusion.151
  781.7 1.7 fusion.155
  784.8 1.7 fusion.158
  788.5 1.8 constant_dynamic-slice_fusion.2
  790.4 1.7 fusion.146
  793.1 2.4 copy.287
  795.5 2.2 multiply_reduce_fusion.3
  798.4 1.7 fusion.151
  801.4 1.7 fusion.155
  804.4 1.7 fusion.158
  808.2 1.8 constant_dynamic-slice_fusion.2
  810.0 1.7 fusion.146
  812.7 2.4 copy.287
  815.1 2.2 multiply_reduce_fusion.3
  818.0 1.7 fusion.151
  (184 shorter events, 28.9 us)
Async XLA Ops:
  0.0 96.9 %copy-start = (bf16[2,32,65536]{2,1,0:T(8,128)(2,1)S(1)}, bf16[2,32,65536]{2,1,0:T(8,128)(2,1)}, u32[]{:S(2)}) copy-start(bf16[2,32,65536]{2,1,0:T(8,128)(2,1)} %param.5) | copy-start | bytes 25165828
  7.4 89.6 %collective-permute-start = (bf16[2,32,61440]{2,1,0:T(8,128)(2,1)}, bf16[2,32,61440]{2,1,0:T(8,128)(2,1)S(1)}, u32[]{:S(2)}, u32[]{:S(2)}) collective-permute-start(bf16[2,32,61440]{2,1,0:T(8,128)(2,1)} %slice.204), channel_id=1, source_target_pairs={{0,1},{1,2},{2,3},{3,4},{4,5},{5,6},{6,7},{8,9},{9,10},{10,11},{11... | collective-permute-start | bytes 23592968 | tf_op jit(solution)/shard_map/ppermute | solution.py:15
  498.6 9.0 %copy-start.1 = (f32[512]{0:T(512)S(1)}, f32[512]{0:T(512)}, u32[]{:S(2)}) copy-start(f32[512]{0:T(512)} %param.7) | copy-start | bytes 6148
  498.6 109.6 %all-to-all-start = ((bf16[128,2,16384]{2,1,0:T(2,128)(2,1)}), bf16[128,2,16384]{2,1,0:T(2,128)(2,1)}, u32[]{:S(2)}, u32[]{:S(2)}) async-start(bf16[128,2,16384]{2,1,0:T(2,128)(2,1)} %reshape.3951), calls=%async_computation | async-start | bytes 16777216 | tf_op jit(solution)/shard_map/all_to_all | solution.py:120
  827.2 0.7 copy-start.2
where the time goes:
time: 845 us; the launch traced here: 828 us
  local copies, waits for them, and re-layouts  344 us (41%)
  waiting for transfers between devices  183 us (22%)
  matrix products  141 us (17%)
  other arithmetic  133 us (16%)
  starting transfers between devices  13.5 us (2%)
  blocking collectives  13.1 us (2%)
    all_to_all x1, waiting for transfers between devices, on_device(): lax.all_to_all(quantized.reshape(2, 1, local_inputs, spectra_here, channe...  101 us
    unnamed x8, local copies, waits for them, and re-layouts  91.7 us
    ppermute x1, waiting for transfers between devices, shifted(): return lax.ppermute(block, axis, route)  82.3 us
    add x1, other arithmetic, on_device(): filtered + taps[tap_index] * extended[:, :, tap_index:tap_index + spectra...  76.6 us
    dot_general x1, matrix products, transform(): jnp.einsum('qkpa,pisan->qiskn', matrix_one, wave, precision=highest)  58.3 us
    convert_element_type x1, local copies, waits for them, and re-layouts, on_device(): quantized = (spectrum * scale[None, :, None, None]).astype(jnp.bfloat16)  54.8 us
    another operation x1, local copies, waits for them, and re-layouts, on_device(): turned.transpose(5, 0, 1, 2, 3, 4)  53.9 us
    another operation x1, local copies, waits for them, and re-layouts, on_device(): by_channel.reshape(owned // block_size, block_size, 2, all_inputs, all_sp...  43.7 us
  transfers between devices with their start and end apart: 2, of which 2 were waited for; matrix products, arithmetic and copies ran while one was open for 0% of the time, Pallas kernels for 0%

commit v1 on v0

v1 whole, which is shorter than its diff:
```python
import functools

import jax
import jax.numpy as jnp
import ml_dtypes
import numpy as np
from jax import lax
from jax.experimental import pallas as pl
from jax.experimental.pallas import tpu as pltpu
from jax.sharding import PartitionSpec as P

ITERS = 4
EPS = 1e-06
TAPS = 16
BEFORE = 7
AFTER = 8
LANES = 128
RADIX = 32
F32 = jnp.float32
BF16 = jnp.bfloat16
MESH = pl.DeviceIdType.MESH


def dft_tables(channels):
    b = np.arange(LANES)
    k = np.arange(RADIX)
    turns = (b[None, :, None] * (k[:, None, None] + RADIX * b[None, None, :])) % channels
    angle = -2.0 * np.pi * turns / channels
    cos, sin = np.cos(angle), np.sin(angle)
    table = np.concatenate(
        [np.concatenate([cos, sin], axis=2), np.concatenate([-sin, cos], axis=2)], axis=1
    ).astype(np.float32)
    high = table.astype(ml_dtypes.bfloat16)
    low = (table - high.astype(np.float32)).astype(ml_dtypes.bfloat16)
    return high, low


def times(z, w):
    re, im = z
    c, s = float(w.real), float(w.imag)
    if abs(s) < 1e-12:
        return (re, im) if c > 0 else (-re, -im)
    if abs(c) < 1e-12:
        return (-im, re) if s > 0 else (im, -re)
    if abs(abs(c) - abs(s)) < 1e-12:
        if c > 0 and s < 0:
            return ((re + im) * c, (im - re) * c)
        if c < 0 and s < 0:
            return ((im - re) * -c, (re + im) * c)
    return (re * c - im * s, re * s + im * c)


def add(x, y):
    return (x[0] + y[0], x[1] + y[1])


def sub(x, y):
    return (x[0] - y[0], x[1] - y[1])


def fft(points):
    size = len(points)
    if size == 1:
        return points
    if size == 2:
        return [add(points[0], points[1]), sub(points[0], points[1])]
    if size == 4:
        even = [add(points[0], points[2]), sub(points[0], points[2])]
        odd = [add(points[1], points[3]), sub(points[1], points[3])]
        turned = (odd[1][1], -odd[1][0])
        return [add(even[0], odd[0]), add(even[1], turned), sub(even[0], odd[0]), sub(even[1], turned)]
    if size == 8:
        even, odd = fft(points[0::2]), fft(points[1::2])
        odd = [times(z, np.exp(-2j * np.pi * i / 8)) for i, z in enumerate(odd)]
        return [add(e, o) for e, o in zip(even, odd)] + [sub(e, o) for e, o in zip(even, odd)]
    outer = size // 4
    result = [None] * size
    firsts = []
    for j in range(outer):
        first = fft([points[j + outer * r] for r in range(4)])
        firsts.append([times(z, np.exp(-2j * np.pi * j * u / size)) for u, z in enumerate(first)])
    for u in range(4):
        second = fft([firsts[j][u] for j in range(outer)])
        for v in range(outer):
            result[u + 4 * v] = second[v]
    return result


def filter_kernel(here, keep_ref, prev_ref, own_ref, next_ref, taps_ref, high_ref, low_ref, spec_ref, power_ref, work):
    group = own_ref.shape[1]
    channels = taps_ref.shape[1]

    def fir(a, carry):
        start = pl.multiple_of(a * LANES, LANES)
        keep = keep_ref[0:1, :]
        for p in range(2):
            rows = [taps_ref[k : k + 1, pl.ds(start, LANES)] for k in range(TAPS)]
            sums = [None] * here
            for j in range(here + TAPS - 1):
                if j < BEFORE:
                    source, spot = prev_ref, j
                elif j < BEFORE + here:
                    source, spot = own_ref, j - BEFORE
                else:
                    source, spot = next_ref, j - BEFORE - here
                at = pl.multiple_of(start + spot * channels, LANES)
                sample = source[p, :, pl.ds(at, LANES)].astype(F32)
                for k in range(TAPS):
                    u = j - k
                    if 0 <= u < here:
                        term = sample * rows[k]
                        sums[u] = term if sums[u] is None else sums[u] + term
                if j == BEFORE + here - 1:
                    for u in range(here - AFTER, here):
                        sums[u] = sums[u] * keep
            for u in range(here):
                work[p, a, u] = sums[u]
        return carry

    lax.fori_loop(0, RADIX, fir, 0)

    def turn(s, carry):
        for half in range(group // 8):
            rows = pl.ds(8 * half, 8)
            points = [(work[0, a, s, rows, :], work[1, a, s, rows, :]) for a in range(RADIX)]
            for k, (re, im) in enumerate(fft(points)):
                work[0, k, s, rows, :] = re
                work[1, k, s, rows, :] = im
        return carry

    lax.fori_loop(0, here, turn, 0)
    power_ref[...] = jnp.zeros(power_ref.shape, F32)

    def second(k, carry):
        both = jnp.concatenate(
            [work[0, k].reshape(here * group, LANES), work[1, k].reshape(here * group, LANES)], axis=1
        )
        high = both.astype(BF16)
        low = (both - high.astype(F32)).astype(BF16)
        table = high_ref[k]
        out = jnp.dot(high, table, preferred_element_type=F32)
        out = out + jnp.dot(low, table, preferred_element_type=F32)
        out = out + jnp.dot(high, low_ref[k], preferred_element_type=F32)
        out = out.reshape(here, group, 2 * LANES)
        spec_ref[k] = out
        square = jnp.sum(out * out, axis=0)
        power_ref[...] += square[:, :LANES] + square[:, LANES:]
        return carry

    lax.fori_loop(0, RADIX, second, 0)


def filter_bank(keep, before, voltages, after, taps):
    inputs = voltages.shape[1]
    channels = taps.shape[1]
    here = voltages.shape[2] // channels
    group = 16
    high, low = dft_tables(channels)
    whole = lambda *shape: pl.BlockSpec(shape, lambda g: (0,) * len(shape), pipeline_mode=pl.Buffered(1))
    part = lambda count: pl.BlockSpec((2, group, count * channels), lambda g: (0, g, 0))
    return pl.pallas_call(
        functools.partial(filter_kernel, here),
        grid=(inputs // group,),
        in_specs=[
            whole(8, LANES),
            part(BEFORE),
            part(here),
            part(AFTER),
            whole(*taps.shape),
            whole(*high.shape),
            whole(*low.shape),
        ],
        out_specs=[
            pl.BlockSpec((RADIX, here, group, 2 * LANES), lambda g: (0, 0, g, 0)),
            pl.BlockSpec((group, LANES), lambda g: (g, 0)),
        ],
        out_shape=[
            jax.ShapeDtypeStruct((RADIX, here, inputs, 2 * LANES), F32),
            jax.ShapeDtypeStruct((inputs, LANES), F32),
        ],
        scratch_shapes=[pltpu.VMEM((2, RADIX, here, group, LANES), F32)],
        compiler_params=pltpu.CompilerParams(vmem_limit_bytes=60 * 2**20),
        name="filter_bank",
    )(keep, before, voltages, after, taps, jnp.asarray(high), jnp.asarray(low))


def solve_kernel(
    stations, blocks,
    spec_ref, scale_ref, model_ref, first_ref,
    out_ref,
    quant, stage, weights, self_power, back_wide, back_narrow, sum_out, sum_in, norm_out, norm_in, gain, rows_ref,
    stage_sem, back_s, back_r, total_s, total_r, sum_s, sum_r, weight_s, weight_r, norm_s, norm_r,
):
    stn, blk = lax.axis_index("stn"), lax.axis_index("blk")
    here, inputs = spec_ref.shape[1], spec_ref.shape[2]
    chunk = RADIX // stations
    quad = RADIX // blocks
    per = quad // chunk

    def peer_stn(offset):
        return lax.rem(stn + offset, stations)

    def peer_blk(offset):
        return lax.rem(blk + offset, blocks)

    barrier = pltpu.get_barrier_semaphore()
    for offset in range(1, stations):
        pl.semaphore_signal(barrier, inc=1, device_id=(peer_stn(offset), blk), device_id_type=MESH)
    for offset in range(1, blocks):
        pl.semaphore_signal(barrier, inc=1, device_id=(stn, peer_blk(offset)), device_id_type=MESH)

    def fetch(k, slot):
        return pltpu.make_async_copy(spec_ref.at[k], stage.at[slot], stage_sem.at[slot])

    fetch(0, 0).start()

    def quantize(k, carry):
        slot = lax.rem(k, 2)

        @pl.when(k + 1 < RADIX)
        def _():
            fetch(k + 1, 1 - slot).start()

        fetch(k, slot).wait()
        scale = scale_ref[...]
        total = jnp.zeros((inputs, LANES), F32)
        for s in range(here):
            for p in range(2):
                value = (stage[slot, s, :, p * LANES : (p + 1) * LANES] * scale).astype(BF16)
                quant[k, p, s] = value
                wide = value.astype(F32)
                total = total + wide * wide
        self_power[k] = total
        return carry

    lax.fori_loop(0, RADIX, quantize, 0)

    def begin(m, carry):
        gain[m, 0] = jnp.ones((inputs, LANES), F32)
        gain[m, 1] = jnp.zeros((inputs, LANES), F32)
        return carry

    lax.fori_loop(0, quad, begin, 0)

    pl.semaphore_wait(barrier, stations + blocks - 2)

    def back_parts(turn):
        return [(back_wide if turn == 0 else back_narrow).at[n] for n in range(3)]

    def back_copy(turn, c, sender):
        back_out, back_in, _ = back_parts(turn)
        return pltpu.make_async_remote_copy(
            src_ref=back_out.at[c], dst_ref=back_in.at[sender], send_sem=back_s.at[c], recv_sem=back_r.at[sender],
            device_id=(c, blk), device_id_type=MESH,
        )

    def total_copy(turn, c, owner):
        _, _, back_sum = back_parts(turn)
        return pltpu.make_async_remote_copy(
            src_ref=back_sum.at[owner], dst_ref=back_sum.at[owner], send_sem=total_s.at[c], recv_sem=total_r.at[owner],
            device_id=(c, blk), device_id_type=MESH,
        )

    def sum_copy(r, sender):
        return pltpu.make_async_remote_copy(
            src_ref=sum_out.at[r], dst_ref=sum_in.at[sender], send_sem=sum_s.at[r], recv_sem=sum_r.at[sender],
            device_id=(stn, r), device_id_type=MESH,
        )

    def weight_copy(r, owner):
        part = weights.at[pl.ds(owner * quad, quad)]
        return pltpu.make_async_remote_copy(
            src_ref=part, dst_ref=part, send_sem=weight_s.at[r], recv_sem=weight_r.at[owner],
            device_id=(stn, r), device_id_type=MESH,
        )

    def norm_copy(turn, c, sender):
        return pltpu.make_async_remote_copy(
            src_ref=norm_out.at[turn], dst_ref=norm_in.at[turn, sender],
            send_sem=norm_s.at[turn, c], recv_sem=norm_r.at[turn, sender],
            device_id=(c, blk), device_id_type=MESH,
        )

    def weight(turn, k, p):
        return model_ref[p] if turn == 0 else weights[k, p].astype(F32)

    def down(turn, k, c, j):
        w_re, w_im = weight(turn, k, 0), weight(turn, k, 1)
        for s in range(here):
            q_re, q_im = quant[k, 0, s].astype(F32), quant[k, 1, s].astype(F32)
            rows_ref[s : s + 1, :] = jnp.sum(q_re * w_re + q_im * w_im, axis=0, keepdims=True)
            rows_ref[here + s : here + s + 1, :] = jnp.sum(q_re * w_im - q_im * w_re, axis=0, keepdims=True)
        back_out = back_parts(turn)[0]
        back_out[c, j] = rows_ref[...].astype(back_out.dtype)

    def up(turn, k, r, j):
        c, jj = lax.div(k, chunk), lax.rem(k, chunk)
        rows_ref[...] = back_parts(turn)[2][c, jj].astype(F32)
        h_re = jnp.zeros((inputs, LANES), F32)
        h_im = jnp.zeros((inputs, LANES), F32)
        for s in range(here):
            q_re, q_im = quant[k, 0, s].astype(F32), quant[k, 1, s].astype(F32)
            b_re, b_im = rows_ref[s : s + 1, :], rows_ref[here + s : here + s + 1, :]
            h_re = h_re + (q_re * b_re - q_im * b_im)
            h_im = h_im + (q_re * b_im + q_im * b_re)
        own = self_power[k]
        sum_out[r, j, 0] = (h_re - own * weight(turn, k, 0)).astype(BF16)
        sum_out[r, j, 1] = (h_im - own * weight(turn, k, 1)).astype(BF16)

    for turn in range(ITERS):
        def down_part(o, carry):
            r = peer_blk(o)
            if turn > 0:

                @pl.when(o > 0)
                def _():
                    weight_copy(r, r).wait_recv()

            def one(n, carry):
                c = r * per + n

                def each(j, carry):
                    down(turn, c * chunk + j, c, j)
                    return carry

                lax.fori_loop(0, chunk, each, 0)

                @pl.when(c != stn)
                def _():
                    back_copy(turn, c, stn).start()

                return carry

            return lax.fori_loop(0, per, one, carry)

        lax.fori_loop(0, blocks, down_part, 0)

        def gather(j, carry):
            back_out, back_in, back_sum = back_parts(turn)
            total = back_out[stn, j].astype(F32)

            def more(o, total):
                return total + back_in[peer_stn(o), j].astype(F32)

            back_sum[stn, j] = lax.fori_loop(1, stations, more, total).astype(back_sum.dtype)
            return carry

        def await_back(o, carry):
            c = peer_stn(o)
            back_copy(turn, c, c).wait_recv()
            return carry

        lax.fori_loop(1, stations, await_back, 0)
        lax.fori_loop(0, chunk, gather, 0)

        def send_total(o, carry):
            total_copy(turn, peer_stn(o), stn).start()
            return carry

        lax.fori_loop(1, stations, send_total, 0)

        def up_part(o, carry):
            r = peer_blk(o)
            for n in range(per):
                c = r * per + n

                @pl.when(c != stn)
                def _():
                    total_copy(turn, c, c).wait_recv()

            def each(j, carry):
                up(turn, r * quad + j, r, j)
                return carry

            lax.fori_loop(0, quad, each, 0)

            @pl.when(o < blocks)
            def _():
                sum_copy(r, blk).start()

            return carry

        lax.fori_loop(1, blocks + 1, up_part, 0)

        def settle(o, carry):
            c = peer_stn(o)
            back_copy(turn, c, stn).wait_send()
            total_copy(turn, c, stn).wait_send()
            if turn > 0:
                norm_copy(turn - 1, c, c).wait_recv()
                norm_copy(turn - 1, c, stn).wait_send()
            return carry

        lax.fori_loop(1, stations, settle, 0)

        def await_sum(o, carry):
            r = peer_blk(o)
            sum_copy(r, r).wait_recv()
            if turn > 0:
                weight_copy(r, blk).wait_send()
            return carry

        lax.fori_loop(1, blocks, await_sum, 0)

        if turn > 0:

            def norms(o, total):
                return total + norm_in[turn - 1, peer_stn(o)]

            rows_ref[0:8, :] = lax.fori_loop(1, stations, norms, norm_out[turn - 1])
        else:
            rows_ref[0:8, :] = first_ref[...]

        for m in range(quad):
            total_re = sum_out[blk, m, 0].astype(F32)
            total_im = sum_out[blk, m, 1].astype(F32)

            def more(o, totals):
                r = peer_blk(o)
                return totals[0] + sum_in[r, m, 0].astype(F32), totals[1] + sum_in[r, m, 1].astype(F32)

            total_re, total_im = lax.fori_loop(1, blocks, more, (total_re, total_im))
            m_re, m_im = model_ref[0], model_ref[1]
            g_re, g_im = gain[m, 0], gain[m, 1]
            w_re = g_re * m_re - g_im * m_im
            w_im = g_re * m_im + g_im * m_re
            denom = rows_ref[m : m + 1, :] - (w_re * w_re + w_im * w_im) + EPS
            new_re = (m_re * total_re + m_im * total_im) / denom
            new_im = (m_re * total_im - m_im * total_re) / denom
            if turn % 2 == 1:
                new_re = (new_re + g_re) * 0.5
                new_im = (new_im + g_im) * 0.5
            if turn == ITERS - 1:
                out_ref[m, 0] = new_re
                out_ref[m, 1] = new_im
            else:
                gain[m, 0] = new_re
                gain[m, 1] = new_im
                w_re = new_re * m_re - new_im * m_im
                w_im = new_re * m_im + new_im * m_re
                weights[blk * quad + m, 0] = w_re.astype(BF16)
                weights[blk * quad + m, 1] = w_im.astype(BF16)
                norm_out[turn, m : m + 1, :] = jnp.sum(w_re * w_re + w_im * w_im, axis=0, keepdims=True)

        if turn < ITERS - 1:
            for m in range(quad, 8):
                norm_out[turn, m : m + 1, :] = jnp.zeros((1, LANES), F32)

            def send_weight(o, carry):
                weight_copy(peer_blk(o), blk).start()
                return carry

            lax.fori_loop(1, blocks, send_weight, 0)

            def send_norm(o, carry):
                norm_copy(turn, peer_stn(o), stn).start()
                return carry

            lax.fori_loop(1, stations, send_norm, 0)

        def sent(o, carry):
            sum_copy(peer_blk(o), blk).wait_send()
            return carry

        lax.fori_loop(1, blocks, sent, 0)


def solve(stations, blocks, spec, scale, model, first):
    here, inputs = spec.shape[1], spec.shape[2]
    chunk, quad = RADIX // stations, RADIX // blocks
    vmem = pl.BlockSpec(memory_space=pltpu.VMEM)
    dma = pltpu.SemaphoreType.DMA
    return pl.pallas_call(
        functools.partial(solve_kernel, stations, blocks),
        in_specs=[pl.BlockSpec(memory_space=pl.ANY), vmem, vmem, vmem],
        out_specs=vmem,
        out_shape=jax.ShapeDtypeStruct((quad, 2, inputs, LANES), F32),
        scratch_shapes=[
            pltpu.VMEM((RADIX, 2, here, inputs, LANES), BF16),
            pltpu.VMEM((2, here, inputs, 2 * LANES), F32),
            pltpu.VMEM((RADIX, 2, inputs, LANES), BF16),
            pltpu.VMEM((RADIX, inputs, LANES), F32),
            pltpu.VMEM((3, stations, chunk, 2 * here, LANES), F32),
            pltpu.VMEM((3, stations, chunk, 2 * here, LANES), BF16),
            pltpu.VMEM((blocks, quad, 2, inputs, LANES), BF16),
            pltpu.VMEM((blocks, quad, 2, inputs, LANES), BF16),
            pltpu.VMEM((ITERS - 1, 8, LANES), F32),
            pltpu.VMEM((ITERS - 1, stations, 8, LANES), F32),
            pltpu.VMEM((quad, 2, inputs, LANES), F32),
            pltpu.VMEM((2 * here, LANES), F32),
            dma((2,)),
            dma((stations,)),
            dma((stations,)),
            dma((stations,)),
            dma((stations,)),
            dma((blocks,)),
            dma((blocks,)),
            dma((blocks,)),
            dma((blocks,)),
            dma((ITERS - 1, stations)),
            dma((ITERS - 1, stations)),
        ],
        compiler_params=pltpu.CompilerParams(
            collective_id=0, has_side_effects=True, vmem_limit_bytes=40 * 2**20
        ),
        name="gain_solver",
    )(spec, scale, model, first)


def on_device(stations, blocks, voltages, taps, model_phase):
    inputs = voltages.shape[1]
    channels = taps.shape[1]
    here = voltages.shape[2] // channels
    stn, blk = lax.axis_index("stn"), lax.axis_index("blk")
    before = lax.ppermute(
        voltages[:, :, (here - BEFORE) * channels :], "blk", [(i, i + 1) for i in range(blocks - 1)]
    )
    after = lax.ppermute(
        voltages[:, :, : AFTER * channels], "blk", [(i, (i - 1) % blocks) for i in range(blocks)]
    )
    keep = jnp.where(blk == blocks - 1, 0.0, 1.0) * jnp.ones((8, LANES), F32)
    spec, power = filter_bank(keep, before, voltages, after, taps)
    total = lax.psum(jnp.sum(power, axis=1), "blk")
    scale = 1.0 / jnp.sqrt(total / (here * blocks * channels) + EPS)
    scale = jnp.broadcast_to(scale[:, None], (inputs, LANES))
    model_re, model_im = jnp.cos(model_phase), jnp.sin(model_phase)
    first = jnp.broadcast_to(jnp.sum(model_re * model_re + model_im * model_im), (8, LANES))
    model = lax.dynamic_slice_in_dim(jnp.stack([model_re, model_im]), stn * inputs, inputs, axis=1)
    model = jnp.broadcast_to(model[:, :, None], (2, inputs, LANES))
    gains = solve(stations, blocks, spec, scale, model, first)
    quad = RADIX // blocks
    moved = lax.all_to_all(
        gains.reshape(quad * 2 * inputs, LANES).T, ("stn", "blk"), split_axis=0, concat_axis=0, tiled=True
    )
    lanes = LANES // (stations * blocks)
    moved = moved.reshape(stations, blocks, lanes, quad, 2, inputs).transpose(4, 2, 1, 3, 0, 5)
    return moved.reshape(2, lanes * RADIX, stations * inputs)


def solution(mesh):
    stations, blocks = mesh.shape["stn"], mesh.shape["blk"]
    in_specs = (P(None, "stn", "blk"), P(), P())
    out_specs = P(None, ("stn", "blk"), None)
    return jax.shard_map(
        functools.partial(on_device, stations, blocks),
        mesh=mesh, in_specs=in_specs, out_specs=out_specs, check_vma=False,
    )
```

time: 845 us -> 276 us (0.33); the launches traced: 828 us -> 275 us
  local copies, waits for them, and re-layouts: 344 us -> 11.7 us
  Pallas kernels: 0 us -> 185 us
  waiting for transfers between devices: 183 us -> 39.7 us
  matrix products: 141 us -> 0 us
  other arithmetic: 133 us -> 1.88 us
  blocking collectives: 13.1 us -> 31.7 us
  starting transfers between devices: 13.5 us -> 4.51 us
    pallas_call x0 -> x2, Pallas kernels: none -> 185 us  [the longest x1 132 us: solve(): pl.pallas_call(functools.partial(solve_kernel, stations, blocks), in_spec...]
    dot_general x34 -> x0, matrix products: 141 us -> none  [the longest x1 58.3 us: transform(): jnp.einsum('qkpa,pisan->qiskn', matrix_one, wave, precision=highest)]
    all_to_all x1 -> x0, waiting for transfers between devices: 101 us -> none  [on_device(): lax.all_to_all(quantized.reshape(2, 1, local_inputs, spectra_here, channe...]
    another operation x6 -> x0, local copies, waits for them, and re-layouts: 97.7 us -> none  [the longest x1 53.9 us: on_device(): turned.transpose(5, 0, 1, 2, 3, 4)]
    unnamed x8 -> x2, local copies, waits for them, and re-layouts: 91.7 us -> 0.01 us
    add x33 -> x0, other arithmetic: 79.3 us -> none  [the longest x1 76.6 us: on_device(): filtered + taps[tap_index] * extended[:, :, tap_index:tap_index + spectra...]
    reshape x3, local copies, waits for them, and re-layouts: 72.4 us -> 1.39 us  [the longest x1 0.87 us: on_device(): return moved.reshape(2, lanes * RADIX, stations * inputs)]
    convert_element_type x1 -> x0, local copies, waits for them, and re-layouts: 54.8 us -> none  [on_device(): quantized = (spectrum * scale[None, :, None, None]).astype(jnp.bfloat16)]
  transfers between devices with their start and end apart: 2 -> 2, of which waited for: 2 -> 2; matrix products, arithmetic and copies ran while one was open for 0% -> 2% of each run, Pallas kernels for 0% -> 0%
where the time goes in v1:
time: 276 us; the launch traced here: 275 us
  Pallas kernels  185 us (67%)
  waiting for transfers between devices  39.7 us (14%)
  blocking collectives  31.7 us (11%)
  local copies, waits for them, and re-layouts  11.7 us (4%)
  starting transfers between devices  4.51 us (2%)
    pallas_call x1, Pallas kernels, solve(): pl.pallas_call(functools.partial(solve_kernel, stations, blocks), in_spec...  132 us
    pallas_call x1, Pallas kernels, filter_bank(): pl.pallas_call(functools.partial(filter_kernel, here), grid=(inputs // gr...  53.4 us
    ppermute x1, waiting for transfers between devices, on_device(): lax.ppermute(voltages[:, :, (here - BEFORE) * channels:], 'blk', [(i, i +...  39.3 us
    all_to_all x1, blocking collectives, on_device(): lax.all_to_all(gains.reshape(quad * 2 * inputs, LANES).T, ('stn', 'blk'),...  18.8 us
    psum x1, blocking collectives, on_device(): total = lax.psum(jnp.sum(power, axis=1), 'blk')  13 us
  transfers between devices with their start and end apart: 2, of which 2 were waited for; matrix products, arithmetic and copies ran while one was open for 2% of the time, Pallas kernels for 0%

profile of v1, /device:TPU:1, one launch (start us, length us, event | category | flops | bytes accessed | tf_op | source)
XLA Modules:
  0.0 275.0 jit_solution(4648207508011074075)
XLA Ops:
  0.0 4.4 %slice.7 = bf16[2,32,32768]{2,1,0:T(8,128)(2,1)} slice(bf16[2,32,65536]{2,1,0:T(8,128)(2,1)} %own_ref.1), slice={[0:2], [0:32], [0:32768]} | slice | bytes 8388608 | tf_op jit(solution)/shard_map/slice | solution.py:519
  4.4 0.0 copy-start
  4.4 1.4 collective-permute-start.1
  5.8 4.1 %slice.6 = bf16[2,32,28672]{2,1,0:T(8,128)(2,1)} slice(bf16[2,32,65536]{2,1,0:T(8,128)(2,1)} %own_ref.1), slice={[0:2], [0:32], [36864:65536]} | slice | bytes 7340032 | tf_op jit(solution)/shard_map/slice | solution.py:516
  9.9 3.1 %collective-permute-start = (bf16[2,32,28672]{2,1,0:T(8,128)(2,1)}, bf16[2,32,28672]{2,1,0:T(8,128)(2,1)}, u32[]{:S(2)}, u32[]{:S(2)}) collective-permute-start(bf16[2,32,28672]{2,1,0:T(8,128)(2,1)} %slice.6), channel_id=1, source_target_pairs={{0,1},{1,2},{2,3},{3,4},{4,5},{5,6},{6,7},{8,9},{9,10},{10,11},{11... | collective-permute-start | bytes 11010056 | tf_op jit(solution)/shard_map/ppermute | solution.py:515
  13.0 0.0 copy-done
  13.1 0.1 fusion
  13.1 0.7 add_reduce_fusion
  13.8 39.3 %collective-permute-done.prev_ref = bf16[2,32,28672]{2,1,0:T(8,128)(2,1)} collective-permute-done((bf16[2,32,28672]{2,1,0:T(8,128)(2,1)}, bf16[2,32,28672]{2,1,0:T(8,128)(2,1)}, u32[]{:S(2)}, u32[]{:S(2)}) %collective-permute-start) | collective-permute-done | bytes 3670048 | tf_op jit(solution)/shard_map/ppermute | solution.py:515
  53.1 0.4 collective-permute-done.1.next_ref
  53.5 0.6 mul.12.keep_ref
  54.1 53.4 %filter_bank.1 = (f32[32,16,32,256]{3,2,1,0:T(8,128)}, f32[32,128]{1,0:T(8,128)}) custom-call(f32[8,128]{1,0:T(8,128)} %mul.12.keep_ref, bf16[2,32,28672]{2,1,0:T(8,128)(2,1)} %collective-permute-done.prev_ref, bf16[2,32,65536]{2,1,0:T(8,128)(2,1)} %own_ref.1, bf16[2,32,32768]{2,1,0:T(8,128)(2,1)} %collective-permute-done.1.next_ref, f32[16,4096]{1,0:T(8,128)} %taps_ref.1, ...), custom_call_target="tpu_custom_call" | custom-call | tf_op jit(solution)/shard_map/filter_bank/pallas_call | solution.py:161
  107.5 0.8 reduce_sum.18
  108.3 13.0 %psum.7 = f32[32]{0:T(128)S(1)} all-reduce(f32[32]{0:T(128)S(1)} %reduce_sum.18), channel_id=1, replica_groups=mesh['stn'=16,'blk'=8] {'blk'}, use_global_device_ids=true, to_apply=%region_1.2 | all-reduce | flops 32 | bytes 256 | tf_op jit(solution)/shard_map/psum | solution.py:523
  121.3 0.1 broadcast_in_dim.6.scale_ref
  121.3 0.1 broadcast_in_dim.7.model_ref
  121.4 0.6 broadcast_in_dim.8.first_ref
  122.1 132.0 %gain_solver.1 = f32[4,2,32,128]{3,2,1,0:T(8,128)S(1)} custom-call(f32[32,16,32,256]{3,2,1,0:T(8,128)} %get-tuple-element.7.spec_ref, f32[32,128]{1,0:T(8,128)S(1)} %broadcast_in_dim.6.scale_ref, f32[2,32,128]{2,1,0:T(8,128)S(1)} %broadcast_in_dim.7.model_ref, f32[8,128]{1,0:T(8,128)S(1)} %broadcast_in_dim.8.first_ref), custom_call_target="tpu_custom_call" | custom-call | tf_op jit(solution)/shard_map/gain_solver/pallas_call | solution.py:473
  254.1 0.1 copy.10
  254.2 0.1 all_to_all.6
  254.3 18.8 %all_to_all.9 = f32[128,1,256]{2,1,0:T(1,128)S(1)} all-to-all(f32[128,1,256]{2,1,0:T(1,128)S(1)} %all_to_all.6), channel_id=1, replica_groups=mesh['stn'=16,'blk'=8] {'stn','blk'}, dimensions={0} | all-to-all | bytes 262144 | tf_op jit(solution)/shard_map/all_to_all | solution.py:532
  273.1 0.3 reduce
  273.4 0.4 reshape.15
  273.8 0.3 copy.11
  274.1 0.9 reshape.16
  (2 shorter events, 0.0 us)
Async XLA Ops:
  4.4 8.6 %copy-start = (f32[512]{0:T(512)S(1)}, f32[512]{0:T(512)}, u32[]{:S(2)}) copy-start(f32[512]{0:T(512)} %param.7) | copy-start | bytes 6148
  4.4 49.1 %collective-permute-start.1 = (bf16[2,32,32768]{2,1,0:T(8,128)(2,1)}, bf16[2,32,32768]{2,1,0:T(8,128)(2,1)}, u32[]{:S(2)}, u32[]{:S(2)}) collective-permute-start(bf16[2,32,32768]{2,1,0:T(8,128)(2,1)} %slice.7), channel_id=1, source_target_pairs={{0,7},{1,0},{2,1},{3,2},{4,3},{5,4},{6,5},{7,6},{8,15},{9,8},{10,9... | collective-permute-start | bytes 12582920 | tf_op jit(solution)/shard_map/ppermute | solution.py:518
  9.9 43.2 %collective-permute-start = (bf16[2,32,28672]{2,1,0:T(8,128)(2,1)}, bf16[2,32,28672]{2,1,0:T(8,128)(2,1)}, u32[]{:S(2)}, u32[]{:S(2)}) collective-permute-start(bf16[2,32,28672]{2,1,0:T(8,128)(2,1)} %slice.6), channel_id=1, source_target_pairs={{0,1},{1,2},{2,3},{3,4},{4,5},{5,6},{6,7},{8,9},{9,10},{10,11},{11... | collective-permute-start | bytes 11010056 | tf_op jit(solution)/shard_map/ppermute | solution.py:515

commit v2 on v1

--- a/solution.py
+++ b/solution.py
@@ -15,6 +15,7 @@
 BEFORE = 7
 AFTER = 8
 LANES = 128
+GROUP = 16
 RADIX = 32
 F32 = jnp.float32
 BF16 = jnp.bfloat16
@@ -86,113 +87,19 @@
     return result
 
 
-def filter_kernel(here, keep_ref, prev_ref, own_ref, next_ref, taps_ref, high_ref, low_ref, spec_ref, power_ref, work):
-    group = own_ref.shape[1]
-    channels = taps_ref.shape[1]
-
-    def fir(a, carry):
-        start = pl.multiple_of(a * LANES, LANES)
-        keep = keep_ref[0:1, :]
-        for p in range(2):
-            rows = [taps_ref[k : k + 1, pl.ds(start, LANES)] for k in range(TAPS)]
-            sums = [None] * here
-            for j in range(here + TAPS - 1):
-                if j < BEFORE:
-                    source, spot = prev_ref, j
-                elif j < BEFORE + here:
-                    source, spot = own_ref, j - BEFORE
-                else:
-                    source, spot = next_ref, j - BEFORE - here
-                at = pl.multiple_of(start + spot * channels, LANES)
-                sample = source[p, :, pl.ds(at, LANES)].astype(F32)
-                for k in range(TAPS):
-                    u = j - k
-                    if 0 <= u < here:
-                        term = sample * rows[k]
-                        sums[u] = term if sums[u] is None else sums[u] + term
-                if j == BEFORE + here - 1:
-                    for u in range(here - AFTER, here):
-                        sums[u] = sums[u] * keep
-            for u in range(here):
-                work[p, a, u] = sums[u]
-        return carry
-
-    lax.fori_loop(0, RADIX, fir, 0)
-
-    def turn(s, carry):
-        for half in range(group // 8):
-            rows = pl.ds(8 * half, 8)
-            points = [(work[0, a, s, rows, :], work[1, a, s, rows, :]) for a in range(RADIX)]
-            for k, (re, im) in enumerate(fft(points)):
-                work[0, k, s, rows, :] = re
-                work[1, k, s, rows, :] = im
-        return carry
-
-    lax.fori_loop(0, here, turn, 0)
-    power_ref[...] = jnp.zeros(power_ref.shape, F32)
-
-    def second(k, carry):
-        both = jnp.concatenate(
-            [work[0, k].reshape(here * group, LANES), work[1, k].reshape(here * group, LANES)], axis=1
-        )
-        high = both.astype(BF16)
-        low = (both - high.astype(F32)).astype(BF16)
-        table = high_ref[k]
-        out = jnp.dot(high, table, preferred_element_type=F32)
-        out = out + jnp.dot(low, table, preferred_element_type=F32)
-        out = out + jnp.dot(high, low_ref[k], preferred_element_type=F32)
-        out = out.reshape(here, group, 2 * LANES)
-        spec_ref[k] = out
-        square = jnp.sum(out * out, axis=0)
-        power_ref[...] += square[:, :LANES] + square[:, LANES:]
-        return carry
-
-    lax.fori_loop(0, RADIX, second, 0)
-
-
-def filter_bank(keep, before, voltages, after, taps):
-    inputs = voltages.shape[1]
-    channels = taps.shape[1]
-    here = voltages.shape[2] // channels
-    group = 16
-    high, low = dft_tables(channels)
-    whole = lambda *shape: pl.BlockSpec(shape, lambda g: (0,) * len(shape), pipeline_mode=pl.Buffered(1))
-    part = lambda count: pl.BlockSpec((2, group, count * channels), lambda g: (0, g, 0))
-    return pl.pallas_call(
-        functools.partial(filter_kernel, here),
-        grid=(inputs // group,),
-        in_specs=[
-            whole(8, LANES),
-            part(BEFORE),
-            part(here),
-            part(AFTER),
-            whole(*taps.shape),
-            whole(*high.shape),
-            whole(*low.shape),
-        ],
-        out_specs=[
-            pl.BlockSpec((RADIX, here, group, 2 * LANES), lambda g: (0, 0, g, 0)),
-            pl.BlockSpec((group, LANES), lambda g: (g, 0)),
-        ],
-        out_shape=[
-            jax.ShapeDtypeStruct((RADIX, here, inputs, 2 * LANES), F32),
-            jax.ShapeDtypeStruct((inputs, LANES), F32),
-        ],
-        scratch_shapes=[pltpu.VMEM((2, RADIX, here, group, LANES), F32)],
-        compiler_params=pltpu.CompilerParams(vmem_limit_bytes=60 * 2**20),
-        name="filter_bank",
-    )(keep, before, voltages, after, taps, jnp.asarray(high), jnp.asarray(low))
-
-
-def solve_kernel(
+def correlator_kernel(
     stations, blocks,
-    spec_ref, scale_ref, model_ref, first_ref,
+    volt_ref, high_hbm, low_hbm, keep_ref, taps_ref, model_ref, first_ref,
     out_ref,
-    quant, stage, weights, self_power, back_wide, back_narrow, sum_out, sum_in, norm_out, norm_in, gain, rows_ref,
-    stage_sem, back_s, back_r, total_s, total_r, sum_s, sum_r, weight_s, weight_r, norm_s, norm_r,
+    own, prev, following, work, high_ref, low_ref, power_out, power_in, scale_ref,
+    quant, weights, self_power, back_wide, back_narrow, sum_out, sum_in, norm_out, norm_in, gain, rows_ref,
+    own_sem, table_sem, halo_s, halo_r, power_s, power_r, back_s, back_r, total_s, total_r, sum_s, sum_r, weight_s, weight_r, norm_s, norm_r,
 ):
     stn, blk = lax.axis_index("stn"), lax.axis_index("blk")
-    here, inputs = spec_ref.shape[1], spec_ref.shape[2]
+    channels = taps_ref.shape[1]
+    inputs = volt_ref.shape[1]
+    here = volt_ref.shape[2] // channels
+    groups = inputs // GROUP
     chunk = RADIX // stations
     quad = RADIX // blocks
     per = quad // chunk
@@ -209,31 +116,172 @@
     for offset in range(1, blocks):
         pl.semaphore_signal(barrier, inc=1, device_id=(stn, peer_blk(offset)), device_id_type=MESH)
 
-    def fetch(k, slot):
-        return pltpu.make_async_copy(spec_ref.at[k], stage.at[slot], stage_sem.at[slot])
-
-    fetch(0, 0).start()
-
-    def quantize(k, carry):
-        slot = lax.rem(k, 2)
-
-        @pl.when(k + 1 < RADIX)
+    def rows_of(g):
+        return pl.ds(pl.multiple_of(g * GROUP, GROUP), GROUP)
+
+    def own_copy(g):
+        return pltpu.make_async_copy(volt_ref.at[:, rows_of(g), :], own.at[:, rows_of(g), :], own_sem.at[g])
+
+    def table_copy(n):
+        pair = ((high_hbm, high_ref), (low_hbm, low_ref))[n]
+        return pltpu.make_async_copy(*pair, table_sem.at[n])
+
+    def forward(g):
+        return pltpu.make_async_remote_copy(
+            src_ref=volt_ref.at[:, rows_of(g), pl.ds((here - BEFORE) * channels, BEFORE * channels)],
+            dst_ref=prev.at[:, rows_of(g), :], send_sem=halo_s.at[0, g], recv_sem=halo_r.at[0, g],
+            device_id=(stn, peer_blk(1)), device_id_type=MESH,
+        )
+
+    def backward(g):
+        return pltpu.make_async_remote_copy(
+            src_ref=volt_ref.at[:, rows_of(g), pl.ds(0, AFTER * channels)],
+            dst_ref=following.at[:, rows_of(g), :], send_sem=halo_s.at[1, g], recv_sem=halo_r.at[1, g],
+            device_id=(stn, peer_blk(blocks - 1)), device_id_type=MESH,
+        )
+
+    for g in range(groups):
+        own_copy(g).start()
+    for n in range(2):
+        table_copy(n).start()
+    pl.semaphore_wait(barrier, stations + blocks - 2)
+    for g in range(groups):
+
+        @pl.when(blk < blocks - 1)
         def _():
-            fetch(k + 1, 1 - slot).start()
-
-        fetch(k, slot).wait()
+            forward(g).start()
+
+        backward(g).start()
+
+    @pl.when(blk == 0)
+    def _():
+        def clear(j, carry):
+            at = pl.ds(pl.multiple_of(j * channels, channels), channels)
+            for p in range(2):
+                prev[p, :, at] = jnp.zeros((inputs, channels), BF16)
+            return carry
+
+        lax.fori_loop(0, BEFORE, clear, 0)
+
+    def tap_rows(start):
+        return [taps_ref[k : k + 1, pl.ds(start, LANES)] for k in range(TAPS)]
+
+    def accumulate(sums, source, g, p, start, first, count, rows):
+        for j in range(first, first + count):
+            at = pl.multiple_of(start + (j - first) * channels, LANES)
+            sample = source[p, rows_of(g), pl.ds(at, LANES)].astype(F32)
+            for k in range(TAPS):
+                u = j - k
+                if 0 <= u < here:
+                    term = sample * rows[k]
+                    sums[u] = term if sums[u] is None else sums[u] + term
+
+    def filter_own(g, carry):
+        own_copy(g).wait()
+
+        def part(a, carry):
+            start = pl.multiple_of(a * LANES, LANES)
+            rows = tap_rows(start)
+            for p in range(2):
+                sums = [None] * here
+                accumulate(sums, own, g, p, start, BEFORE, here, rows)
+                for u in range(here):
+                    work[p, a, u, rows_of(g), :] = sums[u] if u < here - AFTER else sums[u] * keep_ref[0:1, :]
+            return carry
+
+        return lax.fori_loop(0, RADIX, part, carry)
+
+    lax.fori_loop(0, groups, filter_own, 0)
+    for n in range(2):
+        table_copy(n).wait()
+
+    def transform(g, carry):
+        @pl.when(blk > 0)
+        def _():
+            forward(g).wait_recv()
+
+        backward(g).wait_recv()
+
+        def part(a, carry):
+            start = pl.multiple_of(a * LANES, LANES)
+            rows = tap_rows(start)
+            for p in range(2):
+                sums = [work[p, a, u, rows_of(g), :] for u in range(here)]
+                accumulate(sums, prev, g, p, start, 0, BEFORE, rows)
+                accumulate(sums, following, g, p, start, BEFORE + here, AFTER, rows)
+                for u in range(here):
+                    work[p, a, u, rows_of(g), :] = sums[u]
+            return carry
+
+        lax.fori_loop(0, RADIX, part, 0)
+
+        def turn(s, carry):
+            for half in range(GROUP // 8):
+                rows = pl.ds(pl.multiple_of(g * GROUP + 8 * half, 8), 8)
+                points = [(work[0, a, s, rows, :], work[1, a, s, rows, :]) for a in range(RADIX)]
+                for k, (re, im) in enumerate(fft(points)):
+                    work[0, k, s, rows, :] = re
+                    work[1, k, s, rows, :] = im
+            return carry
+
+        lax.fori_loop(0, here, turn, 0)
+
+        def second(k, total):
+            both = jnp.concatenate(
+                [work[p, k, :, rows_of(g), :].reshape(here * GROUP, LANES) for p in range(2)], axis=1
+            )
+            high = both.astype(BF16)
+            low = (both - high.astype(F32)).astype(BF16)
+            table = high_ref[k]
+            out = jnp.dot(high, table, preferred_element_type=F32)
+            out = out + jnp.dot(low, table, preferred_element_type=F32)
+            out = out + jnp.dot(high, low_ref[k], preferred_element_type=F32)
+            out = out.reshape(here, GROUP, 2 * LANES)
+            work[0, k, :, rows_of(g), :] = out[:, :, :LANES]
+            work[1, k, :, rows_of(g), :] = out[:, :, LANES:]
+            square = jnp.sum(out * out, axis=0)
+            return total + square[:, :LANES] + square[:, LANES:]
+
+        total = lax.fori_loop(0, RADIX, second, jnp.zeros((GROUP, LANES), F32))
+        power_out[rows_of(g), :] = jnp.broadcast_to(jnp.sum(total, axis=1, keepdims=True), (GROUP, LANES))
+        return carry
+
+    lax.fori_loop(0, groups, transform, 0)
+
+    def power_copy(r, sender):
+        return pltpu.make_async_remote_copy(
+            src_ref=power_out, dst_ref=power_in.at[sender], send_sem=power_s.at[r], recv_sem=power_r.at[sender],
+            device_id=(stn, r), device_id_type=MESH,
+        )
+
+    for offset in range(1, blocks):
+        power_copy(peer_blk(offset), blk).start()
+    power = power_out[...]
+    for offset in range(1, blocks):
+        r = peer_blk(offset)
+        power_copy(r, r).wait_recv()
+        power = power + power_in[r]
+    scale_ref[...] = 1.0 / jnp.sqrt(power / (here * blocks * channels) + EPS)
+    for offset in range(1, blocks):
+        power_copy(peer_blk(offset), blk).wait_send()
+    for g in range(groups):
+
+        @pl.when(blk < blocks - 1)
+        def _():
+            forward(g).wait_send()
+
+        backward(g).wait_send()
+
+    def quantize(k):
         scale = scale_ref[...]
         total = jnp.zeros((inputs, LANES), F32)
         for s in range(here):
             for p in range(2):
-                value = (stage[slot, s, :, p * LANES : (p + 1) * LANES] * scale).astype(BF16)
+                value = (work[p, k, s] * scale).astype(BF16)
                 quant[k, p, s] = value
                 wide = value.astype(F32)
                 total = total + wide * wide
         self_power[k] = total
-        return carry
-
-    lax.fori_loop(0, RADIX, quantize, 0)
 
     def begin(m, carry):
         gain[m, 0] = jnp.ones((inputs, LANES), F32)
@@ -241,8 +289,6 @@
         return carry
 
     lax.fori_loop(0, quad, begin, 0)
-
-    pl.semaphore_wait(barrier, stations + blocks - 2)
 
     def back_parts(turn):
         return [(back_wide if turn == 0 else back_narrow).at[n] for n in range(3)]
@@ -320,6 +366,8 @@
                 c = r * per + n
 
                 def each(j, carry):
+                    if turn == 0:
+                        quantize(c * chunk + j)
                     down(turn, c * chunk + j, c, j)
                     return carry
 
@@ -465,19 +513,30 @@
         lax.fori_loop(1, blocks, sent, 0)
 
 
-def solve(stations, blocks, spec, scale, model, first):
-    here, inputs = spec.shape[1], spec.shape[2]
+def correlate(stations, blocks, voltages, high, low, keep, taps, model, first):
+    inputs, channels = voltages.shape[1], taps.shape[1]
+    here = voltages.shape[2] // channels
+    groups = inputs // GROUP
     chunk, quad = RADIX // stations, RADIX // blocks
+    hbm = pl.BlockSpec(memory_space=pl.ANY)
     vmem = pl.BlockSpec(memory_space=pltpu.VMEM)
     dma = pltpu.SemaphoreType.DMA
     return pl.pallas_call(
-        functools.partial(solve_kernel, stations, blocks),
-        in_specs=[pl.BlockSpec(memory_space=pl.ANY), vmem, vmem, vmem],
+        functools.partial(correlator_kernel, stations, blocks),
+        in_specs=[hbm, hbm, hbm, vmem, vmem, vmem, vmem],
         out_specs=vmem,
         out_shape=jax.ShapeDtypeStruct((quad, 2, inputs, LANES), F32),
         scratch_shapes=[
+            pltpu.VMEM((2, inputs, here * channels), BF16),
+            pltpu.VMEM((2, inputs, BEFORE * channels), BF16),
+            pltpu.VMEM((2, inputs, AFTER * channels), BF16),
+            pltpu.VMEM((2, RADIX, here, inputs, LANES), F32),
+            pltpu.VMEM(high.shape, BF16),
+            pltpu.VMEM(low.shape, BF16),
+            pltpu.VMEM((inputs, LANES), F32),
+            pltpu.VMEM((blocks, inputs, LANES), F32),
+            pltpu.VMEM((inputs, LANES), F32),
             pltpu.VMEM((RADIX, 2, here, inputs, LANES), BF16),
-            pltpu.VMEM((2, here, inputs, 2 * LANES), F32),
             pltpu.VMEM((RADIX, 2, inputs, LANES), BF16),
             pltpu.VMEM((RADIX, inputs, LANES), F32),
             pltpu.VMEM((3, stations, chunk, 2 * here, LANES), F32),
@@ -488,7 +547,12 @@
             pltpu.VMEM((ITERS - 1, stations, 8, LANES), F32),
             pltpu.VMEM((quad, 2, inputs, LANES), F32),
             pltpu.VMEM((2 * here, LANES), F32),
+            dma((groups,)),
             dma((2,)),
+            dma((2, groups)),
+            dma((2, groups)),
+            dma((blocks,)),
+            dma((blocks,)),
             dma((stations,)),
             dma((stations,)),
             dma((stations,)),
@@ -501,33 +565,23 @@
             dma((ITERS - 1, stations)),
         ],
         compiler_params=pltpu.CompilerParams(
-            collective_id=0, has_side_effects=True, vmem_limit_bytes=40 * 2**20
+            collective_id=0, has_side_effects=True, vmem_limit_bytes=62 * 2**20
         ),
-        name="gain_solver",
-    )(spec, scale, model, first)
+        name="correlator",
+    )(voltages, high, low, keep, taps, model, first)
 
 
 def on_device(stations, blocks, voltages, taps, model_phase):
     inputs = voltages.shape[1]
     channels = taps.shape[1]
-    here = voltages.shape[2] // channels
     stn, blk = lax.axis_index("stn"), lax.axis_index("blk")
-    before = lax.ppermute(
-        voltages[:, :, (here - BEFORE) * channels :], "blk", [(i, i + 1) for i in range(blocks - 1)]
-    )
-    after = lax.ppermute(
-        voltages[:, :, : AFTER * channels], "blk", [(i, (i - 1) % blocks) for i in range(blocks)]
-    )
     keep = jnp.where(blk == blocks - 1, 0.0, 1.0) * jnp.ones((8, LANES), F32)
-    spec, power = filter_bank(keep, before, voltages, after, taps)
-    total = lax.psum(jnp.sum(power, axis=1), "blk")
-    scale = 1.0 / jnp.sqrt(total / (here * blocks * channels) + EPS)
-    scale = jnp.broadcast_to(scale[:, None], (inputs, LANES))
+    high, low = dft_tables(channels)
     model_re, model_im = jnp.cos(model_phase), jnp.sin(model_phase)
     first = jnp.broadcast_to(jnp.sum(model_re * model_re + model_im * model_im), (8, LANES))
     model = lax.dynamic_slice_in_dim(jnp.stack([model_re, model_im]), stn * inputs, inputs, axis=1)
     model = jnp.broadcast_to(model[:, :, None], (2, inputs, LANES))
-    gains = solve(stations, blocks, spec, scale, model, first)
+    gains = correlate(stations, blocks, voltages, jnp.asarray(high), jnp.asarray(low), keep, taps, model, first)
     quad = RADIX // blocks
     moved = lax.all_to_all(
         gains.reshape(quad * 2 * inputs, LANES).T, ("stn", "blk"), split_axis=0, concat_axis=0, tiled=True

time: 276 us -> 213 us (0.77)
  waiting for transfers between devices: 39.7 us -> 0 us
  blocking collectives: 31.7 us -> 18.3 us
  local copies, waits for them, and re-layouts: 11.7 us -> 5.93 us
  starting transfers between devices: 4.51 us -> 0 us
  Pallas kernels: 185 us -> 188 us
    ppermute x2 -> x0, waiting for transfers between devices: 39.7 us -> none  [the longest x1 39.3 us: on_device(): lax.ppermute(voltages[:, :, (here - BEFORE) * channels:], 'blk', [(i, i +...]
    psum x1 -> x0, blocking collectives: 13 us -> none  [on_device(): total = lax.psum(jnp.sum(power, axis=1), 'blk')]
    slice x2 -> x0, local copies, waits for them, and re-layouts: 8.48 us -> none  [the longest x1 4.38 us: on_device(): voltages[:, :, :AFTER * channels]]
    ppermute x2 -> x0, starting transfers between devices: 4.51 us -> none  [the longest x1 3.09 us: on_device(): lax.ppermute(voltages[:, :, (here - BEFORE) * channels:], 'blk', [(i, i +...]
    pallas_call x2 -> x1, Pallas kernels: 185 us -> 188 us  [correlate(): pl.pallas_call(functools.partial(correlator_kernel, stations, blocks), in...]
  transfers between devices with their start and end apart: 2 -> 0, of which waited for: 2 -> 0; matrix products, arithmetic and copies ran while one was open for 2% -> 0% of each run, Pallas kernels for 0% -> 0%
where the time goes in v2:
time: 213 us
  Pallas kernels  188 us (88%)
  blocking collectives  18.3 us (9%)
  local copies, waits for them, and re-layouts  5.93 us (3%)
    pallas_call x1, Pallas kernels, correlate(): pl.pallas_call(functools.partial(correlator_kernel, stations, blocks), in...  188 us
    all_to_all x1, blocking collectives, on_device(): lax.all_to_all(gains.reshape(quad * 2 * inputs, LANES).T, ('stn', 'blk'),...  18.3 us

profile of v2, /device:TPU:1, one launch (start us, length us, event | category | flops | bytes accessed | tf_op | source)
XLA Modules:
  0.0 213.1 jit_solution(5443039144960816934)
XLA Ops:
  0.0 0.7 fusion.1
  0.7 0.6 add_reduce_fusion
  1.3 0.1 fusion
  1.4 0.6 mul.12.keep_ref
  2.0 1.2 broadcast_in_dim.10.first_ref
  3.2 0.7 broadcast_in_dim.4.model_ref
  3.9 187.9 %correlator.1 = f32[4,2,32,128]{3,2,1,0:T(8,128)} custom-call(bf16[2,32,65536]{2,1,0:T(8,128)(2,1)} %volt_ref.1, bf16[32,256,256]{2,1,0:T(8,128)(2,1)} %constant.25.clone.high_hbm, bf16[32,256,256]{2,1,0:T(8,128)(2,1)} %constant.26.clone.low_hbm, f32[8,128]{1,0:T(8,128)} %mul.12.keep_ref, f32[16,4096]{1,0:T(8,128)} %taps_ref.1, ...), custom_call_target="tpu_custom_call" | custom-call | tf_op jit(solution)/shard_map/correlator/pallas_call | solution.py:524
  191.8 1.0 copy.10
  192.8 0.1 all_to_all.6
  192.9 18.3 %all_to_all.9 = f32[128,1,256]{2,1,0:T(1,128)S(1)} all-to-all(f32[128,1,256]{2,1,0:T(1,128)S(1)} %all_to_all.6), channel_id=1, replica_groups=mesh['stn'=16,'blk'=8] {'stn','blk'}, dimensions={0} | all-to-all | bytes 262144 | tf_op jit(solution)/shard_map/all_to_all | solution.py:586
  211.2 0.3 reduce
  211.5 0.4 reshape.14
  212.0 0.3 copy.11
  212.3 0.9 reshape.15

commit v3 on v2

--- a/solution.py
+++ b/solution.py
@@ -89,26 +89,37 @@
 
 def correlator_kernel(
     stations, blocks,
-    volt_ref, high_hbm, low_hbm, keep_ref, taps_ref, model_ref, first_ref,
+    volt_ref, high_hbm, low_hbm, taps_ref, phase_ref, phases_ref,
     out_ref,
-    own, prev, following, work, high_ref, low_ref, power_out, power_in, scale_ref,
-    quant, weights, self_power, back_wide, back_narrow, sum_out, sum_in, norm_out, norm_in, gain, rows_ref,
-    own_sem, table_sem, halo_s, halo_r, power_s, power_r, back_s, back_r, total_s, total_r, sum_s, sum_r, weight_s, weight_r, norm_s, norm_r,
+    own, prev, following, work, high_ref, low_ref, power_out, power_in, scale_ref, model_ref,
+    near, weights, self_power, back_wide, back_narrow, sum_out, sum_in, gain, rows_ref,
+    turned, final_out, final_in, last_out, last_in,
+    own_sem, table_sem, halo_s, halo_r, power_s, power_r, far_s, far_r, back_s, back_r, total_s, total_r,
+    sum_s, sum_r, weight_s, weight_r, final_s, final_r, last_s, last_r,
 ):
     stn, blk = lax.axis_index("stn"), lax.axis_index("blk")
     channels = taps_ref.shape[1]
     inputs = volt_ref.shape[1]
     here = volt_ref.shape[2] // channels
     groups = inputs // GROUP
-    chunk = RADIX // stations
-    quad = RADIX // blocks
+    core, place = lax.rem(blk, 2), lax.div(blk, 2)
+    partner = blk + 1 - 2 * core
+    places = blocks // 2
+    half = RADIX // 2
+    chunk = half // stations
+    quad = half // places
     per = quad // chunk
+    spectra = 2 * here
+    keep = jnp.where(blk == blocks - 1, 0.0, 1.0)
 
     def peer_stn(offset):
         return lax.rem(stn + offset, stations)
 
     def peer_blk(offset):
         return lax.rem(blk + offset, blocks)
+
+    def peer_place(offset):
+        return lax.rem(place + offset, places)
 
     barrier = pltpu.get_barrier_semaphore()
     for offset in range(1, stations):
@@ -186,12 +197,17 @@
                 sums = [None] * here
                 accumulate(sums, own, g, p, start, BEFORE, here, rows)
                 for u in range(here):
-                    work[p, a, u, rows_of(g), :] = sums[u] if u < here - AFTER else sums[u] * keep_ref[0:1, :]
+                    work[p, a, u, rows_of(g), :] = sums[u] if u < here - AFTER else sums[u] * keep
             return carry
 
         return lax.fori_loop(0, RADIX, part, carry)
 
     lax.fori_loop(0, groups, filter_own, 0)
+    model_ref[0] = jnp.cos(phase_ref[...])
+    model_ref[1] = jnp.sin(phase_ref[...])
+    all_re, all_im = jnp.cos(phases_ref[...]), jnp.sin(phases_ref[...])
+    first = jnp.sum(all_re * all_re + all_im * all_im)
+    rows_ref[...] = jnp.zeros(rows_ref.shape, F32)
     for n in range(2):
         table_copy(n).wait()
 
@@ -233,16 +249,18 @@
             high = both.astype(BF16)
             low = (both - high.astype(F32)).astype(BF16)
             table = high_ref[k]
-            out = jnp.dot(high, table, preferred_element_type=F32)
-            out = out + jnp.dot(low, table, preferred_element_type=F32)
-            out = out + jnp.dot(high, low_ref[k], preferred_element_type=F32)
+            out = jnp.dot(
+                jnp.concatenate([high, low, high], axis=1),
+                jnp.concatenate([table, table, low_ref[k]], axis=0),
+                preferred_element_type=F32,
+            )
             out = out.reshape(here, GROUP, 2 * LANES)
             work[0, k, :, rows_of(g), :] = out[:, :, :LANES]
             work[1, k, :, rows_of(g), :] = out[:, :, LANES:]
             square = jnp.sum(out * out, axis=0)
             return total + square[:, :LANES] + square[:, LANES:]
 
-        total = lax.fori_loop(0, RADIX, second, jnp.zeros((GROUP, LANES), F32))
+        total = lax.fori_loop(0, RADIX, second, jnp.zeros((GROUP, LANES), F32), unroll=4)
         power_out[rows_of(g), :] = jnp.broadcast_to(jnp.sum(total, axis=1, keepdims=True), (GROUP, LANES))
         return carry
 
@@ -272,16 +290,41 @@
 
         backward(g).wait_send()
 
+    def far_rows(k, s):
+        return pl.ds(pl.multiple_of((k * here + s) * LANES, LANES), LANES)
+
+    def far_copy(k):
+        part = pl.ds(pl.multiple_of(k * here * LANES, here * LANES), here * LANES)
+        return pltpu.make_async_remote_copy(
+            src_ref=own.at[:, :, part], dst_ref=following.at[:, :, part], send_sem=far_s.at[k], recv_sem=far_r.at[k],
+            device_id=(stn, partner), device_id_type=MESH,
+        )
+
+    def hand_over(k, carry):
+        scale = scale_ref[...]
+        for s in range(here):
+            for p in range(2):
+                own[p, :, far_rows(k, s)] = (work[p, (1 - core) * half + k, s] * scale).astype(BF16)
+        far_copy(k).start()
+        return carry
+
+    lax.fori_loop(0, half, hand_over, 0)
+
     def quantize(k):
+        far_copy(k).wait_recv()
         scale = scale_ref[...]
         total = jnp.zeros((inputs, LANES), F32)
         for s in range(here):
             for p in range(2):
-                value = (work[p, k, s] * scale).astype(BF16)
-                quant[k, p, s] = value
+                value = (work[p, core * half + k, s] * scale).astype(BF16)
+                near[k, p, s] = value
                 wide = value.astype(F32)
-                total = total + wide * wide
+                wider = following[p, :, far_rows(k, s)].astype(F32)
+                total = total + (wide * wide + wider * wider)
         self_power[k] = total
+
+    def sample(k, p, t):
+        return (near[k, p, t] if t < here else following[p, :, far_rows(k, t - here)]).astype(F32)
 
     def begin(m, carry):
         gain[m, 0] = jnp.ones((inputs, LANES), F32)
@@ -310,52 +353,55 @@
     def sum_copy(r, sender):
         return pltpu.make_async_remote_copy(
             src_ref=sum_out.at[r], dst_ref=sum_in.at[sender], send_sem=sum_s.at[r], recv_sem=sum_r.at[sender],
-            device_id=(stn, r), device_id_type=MESH,
+            device_id=(stn, 2 * r + core), device_id_type=MESH,
         )
 
     def weight_copy(r, owner):
         part = weights.at[pl.ds(owner * quad, quad)]
         return pltpu.make_async_remote_copy(
             src_ref=part, dst_ref=part, send_sem=weight_s.at[r], recv_sem=weight_r.at[owner],
-            device_id=(stn, r), device_id_type=MESH,
-        )
-
-    def norm_copy(turn, c, sender):
-        return pltpu.make_async_remote_copy(
-            src_ref=norm_out.at[turn], dst_ref=norm_in.at[turn, sender],
-            send_sem=norm_s.at[turn, c], recv_sem=norm_r.at[turn, sender],
-            device_id=(c, blk), device_id_type=MESH,
-        )
+            device_id=(stn, 2 * r + core), device_id_type=MESH,
+        )
+
+    def split_norm(norm):
+        high = norm.astype(BF16).astype(F32)
+        rows_ref[2 * spectra : 2 * spectra + 1, :] = high
+        rows_ref[2 * spectra + 1 : 2 * spectra + 2, :] = norm - high
 
     def weight(turn, k, p):
         return model_ref[p] if turn == 0 else weights[k, p].astype(F32)
 
     def down(turn, k, c, j):
         w_re, w_im = weight(turn, k, 0), weight(turn, k, 1)
-        for s in range(here):
-            q_re, q_im = quant[k, 0, s].astype(F32), quant[k, 1, s].astype(F32)
-            rows_ref[s : s + 1, :] = jnp.sum(q_re * w_re + q_im * w_im, axis=0, keepdims=True)
-            rows_ref[here + s : here + s + 1, :] = jnp.sum(q_re * w_im - q_im * w_re, axis=0, keepdims=True)
+        for t in range(spectra):
+            q_re, q_im = sample(k, 0, t), sample(k, 1, t)
+            rows_ref[t : t + 1, :] = jnp.sum(q_re * w_re + q_im * w_im, axis=0, keepdims=True)
+            rows_ref[spectra + t : spectra + t + 1, :] = jnp.sum(q_re * w_im - q_im * w_re, axis=0, keepdims=True)
         back_out = back_parts(turn)[0]
-        back_out[c, j] = rows_ref[...].astype(back_out.dtype)
+        if turn == 0:
+            back_out[c, j] = rows_ref[: 2 * spectra, :]
+        else:
+            split_norm(jnp.sum(w_re * w_re + w_im * w_im, axis=0, keepdims=True))
+            back_out[c, j] = rows_ref[...].astype(BF16)
 
     def up(turn, k, r, j):
         c, jj = lax.div(k, chunk), lax.rem(k, chunk)
-        rows_ref[...] = back_parts(turn)[2][c, jj].astype(F32)
+        back = back_parts(turn)[2]
+        rows_ref[: back.shape[2], :] = back[c, jj].astype(F32)
         h_re = jnp.zeros((inputs, LANES), F32)
         h_im = jnp.zeros((inputs, LANES), F32)
-        for s in range(here):
-            q_re, q_im = quant[k, 0, s].astype(F32), quant[k, 1, s].astype(F32)
-            b_re, b_im = rows_ref[s : s + 1, :], rows_ref[here + s : here + s + 1, :]
+        for t in range(spectra):
+            q_re, q_im = sample(k, 0, t), sample(k, 1, t)
+            b_re, b_im = rows_ref[t : t + 1, :], rows_ref[spectra + t : spectra + t + 1, :]
             h_re = h_re + (q_re * b_re - q_im * b_im)
             h_im = h_im + (q_re * b_im + q_im * b_re)
-        own = self_power[k]
-        sum_out[r, j, 0] = (h_re - own * weight(turn, k, 0)).astype(BF16)
-        sum_out[r, j, 1] = (h_im - own * weight(turn, k, 1)).astype(BF16)
+        own_power = self_power[k]
+        sum_out[r, j, 0] = (h_re - own_power * weight(turn, k, 0)).astype(BF16)
+        sum_out[r, j, 1] = (h_im - own_power * weight(turn, k, 1)).astype(BF16)
 
     for turn in range(ITERS):
         def down_part(o, carry):
-            r = peer_blk(o)
+            r = peer_place(o)
             if turn > 0:
 
                 @pl.when(o > 0)
@@ -381,7 +427,7 @@
 
             return lax.fori_loop(0, per, one, carry)
 
-        lax.fori_loop(0, blocks, down_part, 0)
+        lax.fori_loop(0, places, down_part, 0)
 
         def gather(j, carry):
             back_out, back_in, back_sum = back_parts(turn)
@@ -390,7 +436,12 @@
             def more(o, total):
                 return total + back_in[peer_stn(o), j].astype(F32)
 
-            back_sum[stn, j] = lax.fori_loop(1, stations, more, total).astype(back_sum.dtype)
+            total = lax.fori_loop(1, stations, more, total)
+            if turn > 0:
+                rows_ref[...] = total
+                split_norm(jnp.sum(rows_ref[2 * spectra : 2 * spectra + 2, :], axis=0, keepdims=True))
+                total = rows_ref[...]
+            back_sum[stn, j] = total.astype(back_sum.dtype)
             return carry
 
         def await_back(o, carry):
@@ -408,7 +459,7 @@
         lax.fori_loop(1, stations, send_total, 0)
 
         def up_part(o, carry):
-            r = peer_blk(o)
+            r = peer_place(o)
             for n in range(per):
                 c = r * per + n
 
@@ -422,110 +473,159 @@
 
             lax.fori_loop(0, quad, each, 0)
 
-            @pl.when(o < blocks)
+            @pl.when(o < places)
             def _():
-                sum_copy(r, blk).start()
-
-            return carry
-
-        lax.fori_loop(1, blocks + 1, up_part, 0)
+                sum_copy(r, place).start()
+
+            return carry
+
+        lax.fori_loop(1, places + 1, up_part, 0)
 
         def settle(o, carry):
             c = peer_stn(o)
             back_copy(turn, c, stn).wait_send()
             total_copy(turn, c, stn).wait_send()
-            if turn > 0:
-                norm_copy(turn - 1, c, c).wait_recv()
-                norm_copy(turn - 1, c, stn).wait_send()
             return carry
 
         lax.fori_loop(1, stations, settle, 0)
 
         def await_sum(o, carry):
-            r = peer_blk(o)
+            r = peer_place(o)
             sum_copy(r, r).wait_recv()
             if turn > 0:
-                weight_copy(r, blk).wait_send()
-            return carry
-
-        lax.fori_loop(1, blocks, await_sum, 0)
-
-        if turn > 0:
-
-            def norms(o, total):
-                return total + norm_in[turn - 1, peer_stn(o)]
-
-            rows_ref[0:8, :] = lax.fori_loop(1, stations, norms, norm_out[turn - 1])
-        else:
-            rows_ref[0:8, :] = first_ref[...]
+                weight_copy(r, place).wait_send()
+            return carry
+
+        lax.fori_loop(1, places, await_sum, 0)
 
         for m in range(quad):
-            total_re = sum_out[blk, m, 0].astype(F32)
-            total_im = sum_out[blk, m, 1].astype(F32)
+            k = place * quad + m
+            total_re = sum_out[place, m, 0].astype(F32)
+            total_im = sum_out[place, m, 1].astype(F32)
 
             def more(o, totals):
-                r = peer_blk(o)
+                r = peer_place(o)
                 return totals[0] + sum_in[r, m, 0].astype(F32), totals[1] + sum_in[r, m, 1].astype(F32)
 
-            total_re, total_im = lax.fori_loop(1, blocks, more, (total_re, total_im))
+            total_re, total_im = lax.fori_loop(1, places, more, (total_re, total_im))
             m_re, m_im = model_ref[0], model_ref[1]
             g_re, g_im = gain[m, 0], gain[m, 1]
             w_re = g_re * m_re - g_im * m_im
             w_im = g_re * m_im + g_im * m_re
-            denom = rows_ref[m : m + 1, :] - (w_re * w_re + w_im * w_im) + EPS
+            if turn == 0:
+                norm = first
+            else:
+                tail = back_narrow[2, lax.div(k, chunk), lax.rem(k, chunk), 2 * spectra :, :].astype(F32)
+                norm = tail[0:1, :] + tail[1:2, :]
+            denom = norm - (w_re * w_re + w_im * w_im) + EPS
             new_re = (m_re * total_re + m_im * total_im) / denom
             new_im = (m_re * total_im - m_im * total_re) / denom
             if turn % 2 == 1:
                 new_re = (new_re + g_re) * 0.5
                 new_im = (new_im + g_im) * 0.5
-            if turn == ITERS - 1:
-                out_ref[m, 0] = new_re
-                out_ref[m, 1] = new_im
-            else:
-                gain[m, 0] = new_re
-                gain[m, 1] = new_im
+            gain[m, 0] = new_re
+            gain[m, 1] = new_im
+            if turn < ITERS - 1:
                 w_re = new_re * m_re - new_im * m_im
                 w_im = new_re * m_im + new_im * m_re
-                weights[blk * quad + m, 0] = w_re.astype(BF16)
-                weights[blk * quad + m, 1] = w_im.astype(BF16)
-                norm_out[turn, m : m + 1, :] = jnp.sum(w_re * w_re + w_im * w_im, axis=0, keepdims=True)
+                weights[k, 0] = w_re.astype(BF16)
+                weights[k, 1] = w_im.astype(BF16)
 
         if turn < ITERS - 1:
-            for m in range(quad, 8):
-                norm_out[turn, m : m + 1, :] = jnp.zeros((1, LANES), F32)
-
             def send_weight(o, carry):
-                weight_copy(peer_blk(o), blk).start()
+                weight_copy(peer_place(o), place).start()
                 return carry
 
-            lax.fori_loop(1, blocks, send_weight, 0)
-
-            def send_norm(o, carry):
-                norm_copy(turn, peer_stn(o), stn).start()
-                return carry
-
-            lax.fori_loop(1, stations, send_norm, 0)
+            lax.fori_loop(1, places, send_weight, 0)
 
         def sent(o, carry):
-            sum_copy(peer_blk(o), blk).wait_send()
-            return carry
-
-        lax.fori_loop(1, blocks, sent, 0)
-
-
-def correlate(stations, blocks, voltages, high, low, keep, taps, model, first):
+            sum_copy(peer_place(o), place).wait_send()
+            return carry
+
+        lax.fori_loop(1, places, sent, 0)
+
+    def handed(k, carry):
+        far_copy(k).wait_send()
+        return carry
+
+    lax.fori_loop(0, half, handed, 0)
+
+    def final_copy(r, sender):
+        return pltpu.make_async_remote_copy(
+            src_ref=final_out.at[r], dst_ref=final_in.at[sender], send_sem=final_s.at[r], recv_sem=final_r.at[sender],
+            device_id=(stn, r), device_id_type=MESH,
+        )
+
+    def last_copy(c, sender):
+        return pltpu.make_async_remote_copy(
+            src_ref=last_out.at[c], dst_ref=last_in.at[sender], send_sem=last_s.at[c], recv_sem=last_r.at[sender],
+            device_id=(c, blk), device_id_type=MESH,
+        )
+
+    width = quad * 2 * inputs
+    turned[...] = gain[...].reshape(width, LANES).T.reshape(stations, blocks, width)
+    for r in range(blocks):
+        final_out[r] = turned[:, r, :]
+    for offset in range(1, blocks):
+        final_copy(peer_blk(offset), blk).start()
+    final_in[blk] = final_out[blk]
+    for offset in range(1, blocks):
+        r = peer_blk(offset)
+        final_copy(r, r).wait_recv()
+    for c in range(stations):
+        last_out[c] = final_in[:, c, :]
+
+    def send_last(o, carry):
+        last_copy(peer_stn(o), stn).start()
+        return carry
+
+    lax.fori_loop(1, stations, send_last, 0)
+    last_in[stn] = last_out[stn]
+
+    def await_last(o, carry):
+        c = peer_stn(o)
+        last_copy(c, c).wait_recv()
+        return carry
+
+    lax.fori_loop(1, stations, await_last, 0)
+    span = LANES // inputs
+    for m in range(quad):
+        for p in range(2):
+            at = (2 * m + p) * inputs
+            for n in range(stations // span):
+                block = jnp.concatenate(
+                    [last_in[n * span + i, :, at : at + inputs] for i in range(span)], axis=1
+                )
+                for r in range(blocks):
+                    k = (r % 2) * half + (r // 2) * quad + m
+                    out_ref[p, k : k + 1, n * LANES : (n + 1) * LANES] = block[r : r + 1, :]
+
+    for offset in range(1, blocks):
+        final_copy(peer_blk(offset), blk).wait_send()
+
+    def sent_last(o, carry):
+        last_copy(peer_stn(o), stn).wait_send()
+        return carry
+
+    lax.fori_loop(1, stations, sent_last, 0)
+
+
+def correlate(stations, blocks, voltages, high, low, taps, phase, phases):
     inputs, channels = voltages.shape[1], taps.shape[1]
     here = voltages.shape[2] // channels
     groups = inputs // GROUP
-    chunk, quad = RADIX // stations, RADIX // blocks
+    places, half = blocks // 2, RADIX // 2
+    chunk, quad = half // stations, half // places
+    rows = 4 * here + 16
+    width = quad * 2 * inputs
     hbm = pl.BlockSpec(memory_space=pl.ANY)
     vmem = pl.BlockSpec(memory_space=pltpu.VMEM)
     dma = pltpu.SemaphoreType.DMA
     return pl.pallas_call(
         functools.partial(correlator_kernel, stations, blocks),
-        in_specs=[hbm, hbm, hbm, vmem, vmem, vmem, vmem],
+        in_specs=[hbm, hbm, hbm, vmem, vmem, vmem],
         out_specs=vmem,
-        out_shape=jax.ShapeDtypeStruct((quad, 2, inputs, LANES), F32),
+        out_shape=jax.ShapeDtypeStruct((2, RADIX, stations * inputs), F32),
         scratch_shapes=[
             pltpu.VMEM((2, inputs, here * channels), BF16),
             pltpu.VMEM((2, inputs, BEFORE * channels), BF16),
@@ -536,59 +636,56 @@
             pltpu.VMEM((inputs, LANES), F32),
             pltpu.VMEM((blocks, inputs, LANES), F32),
             pltpu.VMEM((inputs, LANES), F32),
-            pltpu.VMEM((RADIX, 2, here, inputs, LANES), BF16),
-            pltpu.VMEM((RADIX, 2, inputs, LANES), BF16),
-            pltpu.VMEM((RADIX, inputs, LANES), F32),
-            pltpu.VMEM((3, stations, chunk, 2 * here, LANES), F32),
-            pltpu.VMEM((3, stations, chunk, 2 * here, LANES), BF16),
-            pltpu.VMEM((blocks, quad, 2, inputs, LANES), BF16),
-            pltpu.VMEM((blocks, quad, 2, inputs, LANES), BF16),
-            pltpu.VMEM((ITERS - 1, 8, LANES), F32),
-            pltpu.VMEM((ITERS - 1, stations, 8, LANES), F32),
+            pltpu.VMEM((2, inputs, LANES), F32),
+            pltpu.VMEM((half, 2, here, inputs, LANES), BF16),
+            pltpu.VMEM((half, 2, inputs, LANES), BF16),
+            pltpu.VMEM((half, inputs, LANES), F32),
+            pltpu.VMEM((3, stations, chunk, 4 * here, LANES), F32),
+            pltpu.VMEM((3, stations, chunk, rows, LANES), BF16),
+            pltpu.VMEM((places, quad, 2, inputs, LANES), BF16),
+            pltpu.VMEM((places, quad, 2, inputs, LANES), BF16),
             pltpu.VMEM((quad, 2, inputs, LANES), F32),
-            pltpu.VMEM((2 * here, LANES), F32),
+            pltpu.VMEM((rows, LANES), F32),
+            pltpu.VMEM((stations, blocks, width), F32),
+            pltpu.VMEM((blocks, stations, width), F32),
+            pltpu.VMEM((blocks, stations, width), F32),
+            pltpu.VMEM((stations, blocks, width), F32),
+            pltpu.VMEM((stations, blocks, width), F32),
             dma((groups,)),
             dma((2,)),
             dma((2, groups)),
             dma((2, groups)),
             dma((blocks,)),
             dma((blocks,)),
+            dma((half,)),
+            dma((half,)),
             dma((stations,)),
             dma((stations,)),
             dma((stations,)),
             dma((stations,)),
+            dma((places,)),
+            dma((places,)),
+            dma((places,)),
+            dma((places,)),
             dma((blocks,)),
             dma((blocks,)),
-            dma((blocks,)),
-            dma((blocks,)),
-            dma((ITERS - 1, stations)),
-            dma((ITERS - 1, stations)),
+            dma((stations,)),
+            dma((stations,)),
         ],
         compiler_params=pltpu.CompilerParams(
             collective_id=0, has_side_effects=True, vmem_limit_bytes=62 * 2**20
         ),
         name="correlator",
-    )(voltages, high, low, keep, taps, model, first)
+    )(voltages, high, low, taps, phase, phases)
 
 
 def on_device(stations, blocks, voltages, taps, model_phase):
     inputs = voltages.shape[1]
-    channels = taps.shape[1]
-    stn, blk = lax.axis_index("stn"), lax.axis_index("blk")
-    keep = jnp.where(blk == blocks - 1, 0.0, 1.0) * jnp.ones((8, LANES), F32)
-    high, low = dft_tables(channels)
-    model_re, model_im = jnp.cos(model_phase), jnp.sin(model_phase)
-    first = jnp.broadcast_to(jnp.sum(model_re * model_re + model_im * model_im), (8, LANES))
-    model = lax.dynamic_slice_in_dim(jnp.stack([model_re, model_im]), stn * inputs, inputs, axis=1)
-    model = jnp.broadcast_to(model[:, :, None], (2, inputs, LANES))
-    gains = correlate(stations, blocks, voltages, jnp.asarray(high), jnp.asarray(low), keep, taps, model, first)
-    quad = RADIX // blocks
-    moved = lax.all_to_all(
-        gains.reshape(quad * 2 * inputs, LANES).T, ("stn", "blk"), split_axis=0, concat_axis=0, tiled=True
-    )
-    lanes = LANES // (stations * blocks)
-    moved = moved.reshape(stations, blocks, lanes, quad, 2, inputs).transpose(4, 2, 1, 3, 0, 5)
-    return moved.reshape(2, lanes * RADIX, stations * inputs)
+    high, low = dft_tables(taps.shape[1])
+    phase = lax.dynamic_slice_in_dim(model_phase, lax.axis_index("stn") * inputs, inputs)
+    phase = jnp.broadcast_to(phase[:, None], (inputs, LANES))
+    phases = model_phase.reshape(-1, LANES)
+    return correlate(stations, blocks, voltages, jnp.asarray(high), jnp.asarray(low), taps, phase, phases)
 
 
 def solution(mesh):

time: 213 us -> 188 us (0.88)
  blocking collectives: 18.3 us -> 0 us
  Pallas kernels: 188 us -> 185 us
  local copies, waits for them, and re-layouts: 5.93 us -> 3 us
    all_to_all x1 -> x0, blocking collectives: 18.3 us -> none  [on_device(): lax.all_to_all(gains.reshape(quad * 2 * inputs, LANES).T, ('stn', 'blk'),...]
    pallas_call x1, Pallas kernels: 188 us -> 185 us  [correlate(): pl.pallas_call(functools.partial(correlator_kernel, stations, blocks), in...]
    reshape x3 -> x0, local copies, waits for them, and re-layouts: 2.29 us -> none  [the longest x1 1 us: on_device(): gains.reshape(quad * 2 * inputs, LANES)]
where the time goes in v3:
time: 188 us
  Pallas kernels  185 us (98%)
  local copies, waits for them, and re-layouts  3 us (2%)
    pallas_call x1, Pallas kernels, correlate(): pl.pallas_call(functools.partial(correlator_kernel, stations, blocks), in...  185 us

profile of v3, /device:TPU:1, one launch (start us, length us, event | category | flops | bytes accessed | tf_op | source)
XLA Modules:
  0.0 188.2 jit_solution(13535765037883262569)
XLA Ops:
  0.0 0.8 dynamic_slice.3
  0.8 0.7 broadcast_in_dim.2.phase_ref
  1.4 185.2 %correlator.1 = f32[2,32,512]{2,1,0:T(8,128)} custom-call(bf16[2,32,65536]{2,1,0:T(8,128)(2,1)} %volt_ref.1, bf16[32,256,256]{2,1,0:T(8,128)(2,1)} %constant.16.clone.high_hbm, bf16[32,256,256]{2,1,0:T(8,128)(2,1)} %constant.17.clone.low_hbm, f32[16,4096]{1,0:T(8,128)} %taps_ref.1, f32[32,128]{1,0:T(8,128)} %broadcast_in_dim.2.phase_ref, f32[4,128]{1,0:T(4,128)} %bitcast.1), custom_call_target="tpu_custom_call" | custom-call | tf_op jit(solution)/shard_map/correlator/pallas_call | solution.py:624
  186.6 1.6 copy.7

commit v4 on v3

--- a/solution.py
+++ b/solution.py
@@ -89,7 +89,7 @@
 
 def correlator_kernel(
     stations, blocks,
-    volt_ref, high_hbm, low_hbm, taps_ref, phase_ref, phases_ref,
+    volt_ref, high_hbm, low_hbm, taps_ref, phases_ref,
     out_ref,
     own, prev, following, work, high_ref, low_ref, power_out, power_in, scale_ref, model_ref,
     near, weights, self_power, back_wide, back_narrow, sum_out, sum_in, gain, rows_ref,
@@ -203,48 +203,55 @@
         return lax.fori_loop(0, RADIX, part, carry)
 
     lax.fori_loop(0, groups, filter_own, 0)
-    model_ref[0] = jnp.cos(phase_ref[...])
-    model_ref[1] = jnp.sin(phase_ref[...])
+    span = LANES // inputs
+    row = phases_ref[pl.ds(lax.div(stn, span), 1), :]
+    lane = lax.broadcasted_iota(jnp.int32, (inputs, LANES), 1)
+    wanted = lax.broadcasted_iota(jnp.int32, (inputs, LANES), 0) + lax.rem(stn, span) * inputs
+    phase = jnp.sum(jnp.where(lane == wanted, row, 0.0), axis=1, keepdims=True)
+    phase = jnp.broadcast_to(phase, (inputs, LANES))
+    model_ref[0] = jnp.cos(phase)
+    model_ref[1] = jnp.sin(phase)
     all_re, all_im = jnp.cos(phases_ref[...]), jnp.sin(phases_ref[...])
     first = jnp.sum(all_re * all_re + all_im * all_im)
     rows_ref[...] = jnp.zeros(rows_ref.shape, F32)
     for n in range(2):
         table_copy(n).wait()
 
-    def transform(g, carry):
-        @pl.when(blk > 0)
-        def _():
-            forward(g).wait_recv()
-
-        backward(g).wait_recv()
-
-        def part(a, carry):
+    def filter_rest(g, low_half, high_half):
+        spots = [u for u in range(here) if (u < AFTER and low_half) or (u >= AFTER and high_half)]
+
+        def part(a, total):
             start = pl.multiple_of(a * LANES, LANES)
             rows = tap_rows(start)
             for p in range(2):
-                sums = [work[p, a, u, rows_of(g), :] for u in range(here)]
-                accumulate(sums, prev, g, p, start, 0, BEFORE, rows)
-                accumulate(sums, following, g, p, start, BEFORE + here, AFTER, rows)
-                for u in range(here):
+                sums = [work[p, a, u, rows_of(g), :] if u in spots else None for u in range(here)]
+                if low_half:
+                    accumulate(sums, prev, g, p, start, 0, BEFORE, rows)
+                if high_half:
+                    accumulate(sums, following, g, p, start, BEFORE + here, AFTER, rows)
+                for u in spots:
                     work[p, a, u, rows_of(g), :] = sums[u]
-            return carry
-
-        lax.fori_loop(0, RADIX, part, 0)
-
+                    total = total + sums[u] * sums[u]
+            return total
+
+        return lax.fori_loop(0, RADIX, part, jnp.zeros((GROUP, LANES), F32))
+
+    def transform(g, first_spot, count):
         def turn(s, carry):
-            for half in range(GROUP // 8):
-                rows = pl.ds(pl.multiple_of(g * GROUP + 8 * half, 8), 8)
+            for part in range(GROUP // 8):
+                rows = pl.ds(g * GROUP + 8 * part, 8)
                 points = [(work[0, a, s, rows, :], work[1, a, s, rows, :]) for a in range(RADIX)]
                 for k, (re, im) in enumerate(fft(points)):
                     work[0, k, s, rows, :] = re
                     work[1, k, s, rows, :] = im
             return carry
 
-        lax.fori_loop(0, here, turn, 0)
-
-        def second(k, total):
+        lax.fori_loop(first_spot, first_spot + count, turn, 0)
+
+        def second(k, carry):
+            spots = pl.ds(first_spot, count)
             both = jnp.concatenate(
-                [work[p, k, :, rows_of(g), :].reshape(here * GROUP, LANES) for p in range(2)], axis=1
+                [work[p, k, spots, rows_of(g), :].reshape(count * GROUP, LANES) for p in range(2)], axis=1
             )
             high = both.astype(BF16)
             low = (both - high.astype(F32)).astype(BF16)
@@ -254,17 +261,17 @@
                 jnp.concatenate([table, table, low_ref[k]], axis=0),
                 preferred_element_type=F32,
             )
-            out = out.reshape(here, GROUP, 2 * LANES)
-            work[0, k, :, rows_of(g), :] = out[:, :, :LANES]
-            work[1, k, :, rows_of(g), :] = out[:, :, LANES:]
-            square = jnp.sum(out * out, axis=0)
-            return total + square[:, :LANES] + square[:, LANES:]
-
-        total = lax.fori_loop(0, RADIX, second, jnp.zeros((GROUP, LANES), F32), unroll=4)
-        power_out[rows_of(g), :] = jnp.broadcast_to(jnp.sum(total, axis=1, keepdims=True), (GROUP, LANES))
-        return carry
-
-    lax.fori_loop(0, groups, transform, 0)
+            out = out.reshape(count, GROUP, 2 * LANES)
+            work[0, k, spots, rows_of(g), :] = out[:, :, :LANES]
+            work[1, k, spots, rows_of(g), :] = out[:, :, LANES:]
+            return carry
+
+        lax.fori_loop(0, RADIX, second, 0, unroll=4)
+
+    def await_prev(g):
+        @pl.when(blk > 0)
+        def _():
+            forward(g).wait_recv()
 
     def power_copy(r, sender):
         return pltpu.make_async_remote_copy(
@@ -272,8 +279,25 @@
             device_id=(stn, r), device_id_type=MESH,
         )
 
-    for offset in range(1, blocks):
-        power_copy(peer_blk(offset), blk).start()
+    for g in range(groups):
+        await_prev(g)
+        if g < groups - 1:
+            backward(g).wait_recv()
+            total = filter_rest(g, True, True)
+        else:
+            total = filter_rest(g, True, False)
+            transform(g, 0, AFTER)
+            backward(g).wait_recv()
+            total = total + filter_rest(g, False, True)
+        total = jnp.sum(total, axis=1, keepdims=True) * channels
+        power_out[g * GROUP : (g + 1) * GROUP, :] = jnp.broadcast_to(total, (GROUP, LANES))
+        if g < groups - 1:
+            transform(g, 0, here)
+        else:
+            for offset in range(1, blocks):
+                power_copy(peer_blk(offset), blk).start()
+            transform(g, AFTER, here - AFTER)
+
     power = power_out[...]
     for offset in range(1, blocks):
         r = peer_blk(offset)
@@ -588,7 +612,6 @@
         return carry
 
     lax.fori_loop(1, stations, await_last, 0)
-    span = LANES // inputs
     for m in range(quad):
         for p in range(2):
             at = (2 * m + p) * inputs
@@ -610,7 +633,7 @@
     lax.fori_loop(1, stations, sent_last, 0)
 
 
-def correlate(stations, blocks, voltages, high, low, taps, phase, phases):
+def correlate(stations, blocks, voltages, high, low, taps, phases):
     inputs, channels = voltages.shape[1], taps.shape[1]
     here = voltages.shape[2] // channels
     groups = inputs // GROUP
@@ -623,7 +646,7 @@
     dma = pltpu.SemaphoreType.DMA
     return pl.pallas_call(
         functools.partial(correlator_kernel, stations, blocks),
-        in_specs=[hbm, hbm, hbm, vmem, vmem, vmem],
+        in_specs=[hbm, hbm, hbm, vmem, vmem],
         out_specs=vmem,
         out_shape=jax.ShapeDtypeStruct((2, RADIX, stations * inputs), F32),
         scratch_shapes=[
@@ -676,16 +699,13 @@
             collective_id=0, has_side_effects=True, vmem_limit_bytes=62 * 2**20
         ),
         name="correlator",
-    )(voltages, high, low, taps, phase, phases)
+    )(voltages, high, low, taps, phases)
 
 
 def on_device(stations, blocks, voltages, taps, model_phase):
-    inputs = voltages.shape[1]
     high, low = dft_tables(taps.shape[1])
-    phase = lax.dynamic_slice_in_dim(model_phase, lax.axis_index("stn") * inputs, inputs)
-    phase = jnp.broadcast_to(phase[:, None], (inputs, LANES))
     phases = model_phase.reshape(-1, LANES)
-    return correlate(stations, blocks, voltages, jnp.asarray(high), jnp.asarray(low), taps, phase, phases)
+    return correlate(stations, blocks, voltages, jnp.asarray(high), jnp.asarray(low), taps, phases)
 
 
 def solution(mesh):

time: 188 us -> 180 us (0.957)
  Pallas kernels: 185 us -> 179 us
    pallas_call x1, Pallas kernels: 185 us -> 179 us  [correlate(): pl.pallas_call(functools.partial(correlator_kernel, stations, blocks), in...]
where the time goes in v4:
time: 180 us
  Pallas kernels  179 us (99%)
    pallas_call x1, Pallas kernels, correlate(): pl.pallas_call(functools.partial(correlator_kernel, stations, blocks), in...  179 us

profile of v4, /device:TPU:1, one launch (start us, length us, event | category | flops | bytes accessed | tf_op | source)
XLA Modules:
  0.0 180.2 jit_solution(17045203464364125218)
XLA Ops:
  0.0 178.7 %correlator.1 = f32[2,32,512]{2,1,0:T(8,128)} custom-call(bf16[2,32,65536]{2,1,0:T(8,128)(2,1)} %volt_ref.1, bf16[32,256,256]{2,1,0:T(8,128)(2,1)} %constant.4.clone.high_hbm, bf16[32,256,256]{2,1,0:T(8,128)(2,1)} %constant.5.clone.low_hbm, f32[16,4096]{1,0:T(8,128)} %taps_ref.1, f32[4,128]{1,0:T(4,128)} %bitcast.1), custom_call_target="tpu_custom_call" | custom-call | tf_op jit(solution)/shard_map/correlator/pallas_call | solution.py:647
  178.7 1.6 copy.7

commit v5 on v4

--- a/solution.py
+++ b/solution.py
@@ -1,4 +1,5 @@
 import functools
+import math
 
 import jax
 import jax.numpy as jnp
@@ -121,6 +122,24 @@
     def peer_place(offset):
         return lax.rem(place + offset, places)
 
+    side = math.isqrt(stations)
+    row_at, column_at = lax.div(stn, side), lax.rem(stn, side)
+    ring = [min(d, side - d) for d in range(side)]
+    others = sorted(
+        ((dy, dz) for dy in range(side) for dz in range(side) if dy or dz), key=lambda d: -ring[d[0]] - ring[d[1]]
+    )
+
+    def far_first():
+        for dy, dz in others:
+            yield lax.rem(row_at + dy, side) * side + lax.rem(column_at + dz, side)
+
+    def order(turn, q, n):
+        offset = q + lax.div(q, 2) * (1 - 2 * lax.rem(q, 2)) if places == 4 else q
+        if turn == 0:
+            offset = offset + row_at
+        r = lax.rem(place + offset, places)
+        return r, r * per + lax.rem(n + column_at, per)
+
     barrier = pltpu.get_barrier_semaphore()
     for offset in range(1, stations):
         pl.semaphore_signal(barrier, inc=1, device_id=(peer_stn(offset), blk), device_id_type=MESH)
@@ -324,7 +343,9 @@
             device_id=(stn, partner), device_id_type=MESH,
         )
 
-    def hand_over(k, carry):
+    def hand_over(i, carry):
+        c = order(0, lax.div(i, quad), lax.div(lax.rem(i, quad), chunk))[1]
+        k = c * chunk + lax.rem(i, chunk)
         scale = scale_ref[...]
         for s in range(here):
             for p in range(2):
@@ -425,7 +446,7 @@
 
     for turn in range(ITERS):
         def down_part(o, carry):
-            r = peer_place(o)
+            r = order(turn, o, 0)[0]
             if turn > 0:
 
                 @pl.when(o > 0)
@@ -433,7 +454,7 @@
                     weight_copy(r, r).wait_recv()
 
             def one(n, carry):
-                c = r * per + n
+                c = order(turn, o, n)[1]
 
                 def each(j, carry):
                     if turn == 0:
@@ -453,11 +474,21 @@
 
         lax.fori_loop(0, places, down_part, 0)
 
+        def await_back(o, carry):
+            c = peer_stn(o)
+            back_copy(turn, c, c).wait_recv()
+            return carry
+
+        if chunk > 1:
+            lax.fori_loop(1, stations, await_back, 0)
+
         def gather(j, carry):
             back_out, back_in, back_sum = back_parts(turn)
             total = back_out[stn, j].astype(F32)
 
             def more(o, total):
+                if chunk == 1:
+                    await_back(o, 0)
                 return total + back_in[peer_stn(o), j].astype(F32)
 
             total = lax.fori_loop(1, stations, more, total)
@@ -468,21 +499,11 @@
             back_sum[stn, j] = total.astype(back_sum.dtype)
             return carry
 
-        def await_back(o, carry):
-            c = peer_stn(o)
-            back_copy(turn, c, c).wait_recv()
-            return carry
-
-        lax.fori_loop(1, stations, await_back, 0)
         lax.fori_loop(0, chunk, gather, 0)
-
-        def send_total(o, carry):
-            total_copy(turn, peer_stn(o), stn).start()
-            return carry
-
-        lax.fori_loop(1, stations, send_total, 0)
-
-        def up_part(o, carry):
+        for c in far_first():
+            total_copy(turn, c, stn).start()
+
+        def up_part(o):
             r = peer_place(o)
             for n in range(per):
                 c = r * per + n
@@ -496,14 +517,11 @@
                 return carry
 
             lax.fori_loop(0, quad, each, 0)
-
-            @pl.when(o < places)
-            def _():
+            if o > 0:
                 sum_copy(r, place).start()
 
-            return carry
-
-        lax.fori_loop(1, places + 1, up_part, 0)
+        for o in sorted(range(places), key=lambda o: -min(o, places - o)):
+            up_part(o)
 
         def settle(o, carry):
             c = peer_stn(o)
@@ -556,11 +574,8 @@
                 weights[k, 1] = w_im.astype(BF16)
 
         if turn < ITERS - 1:
-            def send_weight(o, carry):
+            for o in sorted(range(1, places), key=lambda o: -min(o, places - o)):
                 weight_copy(peer_place(o), place).start()
-                return carry
-
-            lax.fori_loop(1, places, send_weight, 0)
 
         def sent(o, carry):
             sum_copy(peer_place(o), place).wait_send()
@@ -590,7 +605,7 @@
     turned[...] = gain[...].reshape(width, LANES).T.reshape(stations, blocks, width)
     for r in range(blocks):
         final_out[r] = turned[:, r, :]
-    for offset in range(1, blocks):
+    for offset in sorted(range(1, blocks), key=lambda o: -min(o, blocks - o)):
         final_copy(peer_blk(offset), blk).start()
     final_in[blk] = final_out[blk]
     for offset in range(1, blocks):
@@ -599,11 +614,8 @@
     for c in range(stations):
         last_out[c] = final_in[:, c, :]
 
-    def send_last(o, carry):
-        last_copy(peer_stn(o), stn).start()
-        return carry
-
-    lax.fori_loop(1, stations, send_last, 0)
+    for c in far_first():
+        last_copy(c, stn).start()
     last_in[stn] = last_out[stn]
 
     def await_last(o, carry):

time: 180 us -> 175 us (0.972)
  Pallas kernels: 179 us -> 173 us
    pallas_call x1, Pallas kernels: 179 us -> 173 us  [correlate(): pl.pallas_call(functools.partial(correlator_kernel, stations, blocks), in...]
where the time goes in v5:
time: 175 us; the launch traced here: 174 us
  Pallas kernels  173 us (99%)
    pallas_call x1, Pallas kernels, correlate(): pl.pallas_call(functools.partial(correlator_kernel, stations, blocks), in...  173 us

profile of v5, /device:TPU:1, one launch (start us, length us, event | category | flops | bytes accessed | tf_op | source)
XLA Modules:
  0.0 174.4 jit_solution(905854902326862171)
XLA Ops:
  0.0 172.8 %correlator.1 = f32[2,32,512]{2,1,0:T(8,128)} custom-call(bf16[2,32,65536]{2,1,0:T(8,128)(2,1)} %volt_ref.1, bf16[32,256,256]{2,1,0:T(8,128)(2,1)} %constant.4.clone.high_hbm, bf16[32,256,256]{2,1,0:T(8,128)(2,1)} %constant.5.clone.low_hbm, f32[16,4096]{1,0:T(8,128)} %taps_ref.1, f32[4,128]{1,0:T(4,128)} %bitcast.1), custom_call_target="tpu_custom_call" | custom-call | tf_op jit(solution)/shard_map/correlator/pallas_call | solution.py:659
  172.8 1.6 copy.7

commit v6 on v5

--- a/solution.py
+++ b/solution.py
@@ -93,10 +93,10 @@
     volt_ref, high_hbm, low_hbm, taps_ref, phases_ref,
     out_ref,
     own, prev, following, work, high_ref, low_ref, power_out, power_in, scale_ref, model_ref,
-    near, weights, self_power, back_wide, back_narrow, sum_out, sum_in, gain, rows_ref,
-    turned, final_out, final_in, last_out, last_in,
+    near, weights, self_power, back_wide, back_narrow, sum_out, sum_in, norm_out, norm_in, gain, rows_ref,
+    numer, turned, side_out, side_in, half_out, half_in, final, last_out, last_in,
     own_sem, table_sem, halo_s, halo_r, power_s, power_r, far_s, far_r, back_s, back_r, total_s, total_r,
-    sum_s, sum_r, weight_s, weight_r, final_s, final_r, last_s, last_r,
+    sum_s, sum_r, weight_s, weight_r, norm_s, norm_r, side_s, side_r, half_s, half_r, last_s, last_r,
 ):
     stn, blk = lax.axis_index("stn"), lax.axis_index("blk")
     channels = taps_ref.shape[1]
@@ -401,17 +401,21 @@
             device_id=(stn, 2 * r + core), device_id_type=MESH,
         )
 
-    def weight_copy(r, owner):
-        part = weights.at[pl.ds(owner * quad, quad)]
-        return pltpu.make_async_remote_copy(
-            src_ref=part, dst_ref=part, send_sem=weight_s.at[r], recv_sem=weight_r.at[owner],
+    places_far_first = sorted(range(1, places), key=lambda o: -min(o, places - o))
+
+    def weight_copy(r, owner, m):
+        part = weights.at[owner * quad + m]
+        return pltpu.make_async_remote_copy(
+            src_ref=part, dst_ref=part, send_sem=weight_s.at[r, m], recv_sem=weight_r.at[owner, m],
             device_id=(stn, 2 * r + core), device_id_type=MESH,
         )
 
-    def split_norm(norm):
-        high = norm.astype(BF16).astype(F32)
-        rows_ref[2 * spectra : 2 * spectra + 1, :] = high
-        rows_ref[2 * spectra + 1 : 2 * spectra + 2, :] = norm - high
+    def norm_copy(turn, c, sender):
+        return pltpu.make_async_remote_copy(
+            src_ref=norm_out.at[turn], dst_ref=norm_in.at[turn, sender],
+            send_sem=norm_s.at[turn, c], recv_sem=norm_r.at[turn, sender],
+            device_id=(c, blk), device_id_type=MESH,
+        )
 
     def weight(turn, k, p):
         return model_ref[p] if turn == 0 else weights[k, p].astype(F32)
@@ -423,16 +427,12 @@
             rows_ref[t : t + 1, :] = jnp.sum(q_re * w_re + q_im * w_im, axis=0, keepdims=True)
             rows_ref[spectra + t : spectra + t + 1, :] = jnp.sum(q_re * w_im - q_im * w_re, axis=0, keepdims=True)
         back_out = back_parts(turn)[0]
-        if turn == 0:
-            back_out[c, j] = rows_ref[: 2 * spectra, :]
-        else:
-            split_norm(jnp.sum(w_re * w_re + w_im * w_im, axis=0, keepdims=True))
-            back_out[c, j] = rows_ref[...].astype(BF16)
+        back_out[c, j] = rows_ref[...].astype(back_out.dtype)
 
     def up(turn, k, r, j):
         c, jj = lax.div(k, chunk), lax.rem(k, chunk)
         back = back_parts(turn)[2]
-        rows_ref[: back.shape[2], :] = back[c, jj].astype(F32)
+        rows_ref[...] = back[c, jj].astype(F32)
         h_re = jnp.zeros((inputs, LANES), F32)
         h_im = jnp.zeros((inputs, LANES), F32)
         for t in range(spectra):
@@ -441,22 +441,88 @@
             h_re = h_re + (q_re * b_re - q_im * b_im)
             h_im = h_im + (q_re * b_im + q_im * b_re)
         own_power = self_power[k]
-        sum_out[r, j, 0] = (h_re - own_power * weight(turn, k, 0)).astype(BF16)
-        sum_out[r, j, 1] = (h_im - own_power * weight(turn, k, 1)).astype(BF16)
+        h_re = h_re - own_power * weight(turn, k, 0)
+        h_im = h_im - own_power * weight(turn, k, 1)
+        if turn < ITERS - 1:
+            sum_out[r, j, 0] = h_re.astype(BF16)
+            sum_out[r, j, 1] = h_im.astype(BF16)
+        else:
+            m_re, m_im = model_ref[0], model_ref[1]
+            numer[0, j] = m_re * h_re + m_im * h_im
+            numer[1, j] = m_re * h_im - m_im * h_re
+
+    def side_copy(r, sender):
+        return pltpu.make_async_remote_copy(
+            src_ref=side_out.at[r], dst_ref=side_in.at[sender], send_sem=side_s.at[r], recv_sem=side_r.at[sender],
+            device_id=(stn, r), device_id_type=MESH,
+        )
+
+    def half_copy(r, sender, q):
+        return pltpu.make_async_remote_copy(
+            src_ref=half_out.at[r, q], dst_ref=half_in.at[sender, q],
+            send_sem=half_s.at[r, q], recv_sem=half_r.at[sender, q],
+            device_id=(stn, r), device_id_type=MESH,
+        )
+
+    def last_copy(c, sender):
+        return pltpu.make_async_remote_copy(
+            src_ref=last_out.at[c], dst_ref=last_in.at[sender], send_sem=last_s.at[c], recv_sem=last_r.at[sender],
+            device_id=(c, blk), device_id_type=MESH,
+        )
+
+    blocks_far_first = sorted(range(1, blocks), key=lambda o: -min(o, blocks - o))
+
+    def by_block(value, n):
+        turned[n] = value.reshape(quad * inputs, LANES).T.reshape(stations, blocks, quad * inputs)
+        return [turned[n, :, r, :] for r in range(blocks)]
+
+    def add_norms(turn):
+        def norms(o, total):
+            c = peer_stn(o)
+            norm_copy(turn - 1, c, c).wait_recv()
+            return total + norm_in[turn - 1, c]
+
+        rows_ref[0:8, :] = lax.fori_loop(1, stations, norms, norm_out[turn - 1])
+
+    def denominator(norm, w_re, w_im):
+        return norm - (w_re * w_re + w_im * w_im) + EPS
+
+    def last_side():
+        add_norms(ITERS - 1)
+        m_re, m_im = model_ref[0], model_ref[1]
+        for m in range(quad):
+            g_re, g_im = gain[m, 0], gain[m, 1]
+            w_re = g_re * m_re - g_im * m_im
+            w_im = g_re * m_im + g_im * m_re
+            numer[0, m] = 1.0 / denominator(rows_ref[m : m + 1, :], w_re, w_im)
+        for n, value in enumerate((gain[:, 0], gain[:, 1], numer[0])):
+            for r, part in enumerate(by_block(value, n)):
+                side_out[r, n] = part
+        for offset in blocks_far_first:
+            side_copy(peer_blk(offset), blk).start()
+        side_in[blk] = side_out[blk]
+
+    def send_half(q):
+        for p in range(2):
+            for r, part in enumerate(by_block(numer[p], p)):
+                half_out[r, q, p] = part.astype(BF16)
+        for offset in blocks_far_first:
+            half_copy(peer_blk(offset), blk, q).start()
+        half_in[blk, q] = half_out[blk, q]
 
     for turn in range(ITERS):
         def down_part(o, carry):
             r = order(turn, o, 0)[0]
-            if turn > 0:
-
-                @pl.when(o > 0)
-                def _():
-                    weight_copy(r, r).wait_recv()
-
             def one(n, carry):
                 c = order(turn, o, n)[1]
 
                 def each(j, carry):
+                    if turn > 0:
+
+                        @pl.when(o > 0)
+                        def _():
+                            weight_copy(r, r, lax.rem(c * chunk + j, quad)).wait_recv()
+
                     if turn == 0:
                         quantize(c * chunk + j)
                     down(turn, c * chunk + j, c, j)
@@ -492,16 +558,14 @@
                 return total + back_in[peer_stn(o), j].astype(F32)
 
             total = lax.fori_loop(1, stations, more, total)
-            if turn > 0:
-                rows_ref[...] = total
-                split_norm(jnp.sum(rows_ref[2 * spectra : 2 * spectra + 2, :], axis=0, keepdims=True))
-                total = rows_ref[...]
             back_sum[stn, j] = total.astype(back_sum.dtype)
             return carry
 
         lax.fori_loop(0, chunk, gather, 0)
         for c in far_first():
             total_copy(turn, c, stn).start()
+        if turn == ITERS - 1:
+            last_side()
 
         def up_part(o):
             r = peer_place(o)
@@ -517,7 +581,9 @@
                 return carry
 
             lax.fori_loop(0, quad, each, 0)
-            if o > 0:
+            if turn == ITERS - 1:
+                send_half(r)
+            elif o > 0:
                 sum_copy(r, place).start()
 
         for o in sorted(range(places), key=lambda o: -min(o, places - o)):
@@ -533,12 +599,19 @@
 
         def await_sum(o, carry):
             r = peer_place(o)
-            sum_copy(r, r).wait_recv()
+            if turn < ITERS - 1:
+                sum_copy(r, r).wait_recv()
             if turn > 0:
-                weight_copy(r, place).wait_send()
+                for m in range(quad):
+                    weight_copy(r, place, m).wait_send()
             return carry
 
         lax.fori_loop(1, places, await_sum, 0)
+
+        if turn == ITERS - 1:
+            break
+        if turn > 0:
+            add_norms(turn)
 
         for m in range(quad):
             k = place * quad + m
@@ -557,9 +630,8 @@
             if turn == 0:
                 norm = first
             else:
-                tail = back_narrow[2, lax.div(k, chunk), lax.rem(k, chunk), 2 * spectra :, :].astype(F32)
-                norm = tail[0:1, :] + tail[1:2, :]
-            denom = norm - (w_re * w_re + w_im * w_im) + EPS
+                norm = rows_ref[m : m + 1, :]
+            denom = denominator(norm, w_re, w_im)
             new_re = (m_re * total_re + m_im * total_im) / denom
             new_im = (m_re * total_im - m_im * total_re) / denom
             if turn % 2 == 1:
@@ -567,15 +639,18 @@
                 new_im = (new_im + g_im) * 0.5
             gain[m, 0] = new_re
             gain[m, 1] = new_im
-            if turn < ITERS - 1:
-                w_re = new_re * m_re - new_im * m_im
-                w_im = new_re * m_im + new_im * m_re
-                weights[k, 0] = w_re.astype(BF16)
-                weights[k, 1] = w_im.astype(BF16)
-
-        if turn < ITERS - 1:
-            for o in sorted(range(1, places), key=lambda o: -min(o, places - o)):
-                weight_copy(peer_place(o), place).start()
+            w_re = new_re * m_re - new_im * m_im
+            w_im = new_re * m_im + new_im * m_re
+            weights[k, 0] = w_re.astype(BF16)
+            weights[k, 1] = w_im.astype(BF16)
+            for o in places_far_first:
+                weight_copy(peer_place(o), place, m).start()
+            norm_out[turn, m : m + 1, :] = jnp.sum(w_re * w_re + w_im * w_im, axis=0, keepdims=True)
+
+        for m in range(quad, 8):
+            norm_out[turn, m : m + 1, :] = jnp.zeros((1, LANES), F32)
+        for c in far_first():
+            norm_copy(turn, c, stn).start()
 
         def sent(o, carry):
             sum_copy(peer_place(o), place).wait_send()
@@ -589,31 +664,31 @@
 
     lax.fori_loop(0, half, handed, 0)
 
-    def final_copy(r, sender):
-        return pltpu.make_async_remote_copy(
-            src_ref=final_out.at[r], dst_ref=final_in.at[sender], send_sem=final_s.at[r], recv_sem=final_r.at[sender],
-            device_id=(stn, r), device_id_type=MESH,
-        )
-
-    def last_copy(c, sender):
-        return pltpu.make_async_remote_copy(
-            src_ref=last_out.at[c], dst_ref=last_in.at[sender], send_sem=last_s.at[c], recv_sem=last_r.at[sender],
-            device_id=(c, blk), device_id_type=MESH,
-        )
-
-    width = quad * 2 * inputs
-    turned[...] = gain[...].reshape(width, LANES).T.reshape(stations, blocks, width)
-    for r in range(blocks):
-        final_out[r] = turned[:, r, :]
-    for offset in sorted(range(1, blocks), key=lambda o: -min(o, blocks - o)):
-        final_copy(peer_blk(offset), blk).start()
-    final_in[blk] = final_out[blk]
-    for offset in range(1, blocks):
+    def normed(o, carry):
+        for turn in range(ITERS - 1):
+            norm_copy(turn, peer_stn(o), stn).wait_send()
+        return carry
+
+    lax.fori_loop(1, stations, normed, 0)
+
+    for offset in blocks_far_first:
         r = peer_blk(offset)
-        final_copy(r, r).wait_recv()
+        side_copy(r, r).wait_recv()
+        for q in range(places):
+            half_copy(r, r, q).wait_recv()
+    for half_core in range(2):
+        for q in range(places):
+            owner = 2 * q + half_core
+            for p in range(2):
+                total = half_in[half_core, q, p].astype(F32)
+                for n in range(1, places):
+                    total = total + half_in[2 * n + half_core, q, p].astype(F32)
+                total = total * side_in[owner, 2]
+                if ITERS % 2 == 0:
+                    total = (total + side_in[owner, p]) * 0.5
+                final[(half_core * places + q) * 2 + p] = total
     for c in range(stations):
-        last_out[c] = final_in[:, c, :]
-
+        last_out[c] = final[:, c, :]
     for c in far_first():
         last_copy(c, stn).start()
     last_in[stn] = last_out[stn]
@@ -625,18 +700,22 @@
 
     lax.fori_loop(1, stations, await_last, 0)
     for m in range(quad):
-        for p in range(2):
-            at = (2 * m + p) * inputs
-            for n in range(stations // span):
-                block = jnp.concatenate(
-                    [last_in[n * span + i, :, at : at + inputs] for i in range(span)], axis=1
-                )
-                for r in range(blocks):
-                    k = (r % 2) * half + (r // 2) * quad + m
-                    out_ref[p, k : k + 1, n * LANES : (n + 1) * LANES] = block[r : r + 1, :]
-
-    for offset in range(1, blocks):
-        final_copy(peer_blk(offset), blk).wait_send()
+        for n in range(stations // span):
+            block = jnp.concatenate(
+                [last_in[n * span + i, :, m * inputs : (m + 1) * inputs] for i in range(span)], axis=1
+            )
+            for half_core in range(2):
+                for q in range(places):
+                    for p in range(2):
+                        k = half_core * half + q * quad + m
+                        at = (half_core * places + q) * 2 + p
+                        out_ref[p, k : k + 1, n * LANES : (n + 1) * LANES] = block[at : at + 1, :]
+
+    for offset in blocks_far_first:
+        r = peer_blk(offset)
+        side_copy(r, blk).wait_send()
+        for q in range(places):
+            half_copy(r, blk, q).wait_send()
 
     def sent_last(o, carry):
         last_copy(peer_stn(o), stn).wait_send()
@@ -651,8 +730,7 @@
     groups = inputs // GROUP
     places, half = blocks // 2, RADIX // 2
     chunk, quad = half // stations, half // places
-    rows = 4 * here + 16
-    width = quad * 2 * inputs
+    rows = 4 * here
     hbm = pl.BlockSpec(memory_space=pl.ANY)
     vmem = pl.BlockSpec(memory_space=pltpu.VMEM)
     dma = pltpu.SemaphoreType.DMA
@@ -679,13 +757,19 @@
             pltpu.VMEM((3, stations, chunk, rows, LANES), BF16),
             pltpu.VMEM((places, quad, 2, inputs, LANES), BF16),
             pltpu.VMEM((places, quad, 2, inputs, LANES), BF16),
+            pltpu.VMEM((ITERS - 1, 8, LANES), F32),
+            pltpu.VMEM((ITERS - 1, stations, 8, LANES), F32),
             pltpu.VMEM((quad, 2, inputs, LANES), F32),
             pltpu.VMEM((rows, LANES), F32),
-            pltpu.VMEM((stations, blocks, width), F32),
-            pltpu.VMEM((blocks, stations, width), F32),
-            pltpu.VMEM((blocks, stations, width), F32),
-            pltpu.VMEM((stations, blocks, width), F32),
-            pltpu.VMEM((stations, blocks, width), F32),
+            pltpu.VMEM((2, quad, inputs, LANES), F32),
+            pltpu.VMEM((3, stations, blocks, quad * inputs), F32),
+            pltpu.VMEM((blocks, 3, stations, quad * inputs), F32),
+            pltpu.VMEM((blocks, 3, stations, quad * inputs), F32),
+            pltpu.VMEM((blocks, places, 2, stations, quad * inputs), BF16),
+            pltpu.VMEM((blocks, places, 2, stations, quad * inputs), BF16),
+            pltpu.VMEM((4 * places, stations, quad * inputs), F32),
+            pltpu.VMEM((stations, 4 * places, quad * inputs), F32),
+            pltpu.VMEM((stations, 4 * places, quad * inputs), F32),
             dma((groups,)),
             dma((2,)),
             dma((2, groups)),
@@ -700,10 +784,14 @@
             dma((stations,)),
             dma((places,)),
             dma((places,)),
-            dma((places,)),
-            dma((places,)),
+            dma((places, quad)),
+            dma((places, quad)),
+            dma((ITERS - 1, stations)),
+            dma((ITERS - 1, stations)),
             dma((blocks,)),
             dma((blocks,)),
+            dma((blocks, places)),
+            dma((blocks, places)),
             dma((stations,)),
             dma((stations,)),
         ],

time: 175 us -> 172 us (0.983)
  Pallas kernels: 173 us -> 170 us
    pallas_call x1, Pallas kernels: 173 us -> 170 us  [correlate(): pl.pallas_call(functools.partial(correlator_kernel, stations, blocks), in...]
where the time goes in v6:
time: 172 us
  Pallas kernels  170 us (99%)
    pallas_call x1, Pallas kernels, correlate(): pl.pallas_call(functools.partial(correlator_kernel, stations, blocks), in...  170 us

profile of v6, /device:TPU:1, one launch (start us, length us, event | category | flops | bytes accessed | tf_op | source)
XLA Modules:
  0.0 172.0 jit_solution(13689609240031188641)
XLA Ops:
  0.0 170.4 %correlator.1 = f32[2,32,512]{2,1,0:T(8,128)} custom-call(bf16[2,32,65536]{2,1,0:T(8,128)(2,1)} %volt_ref.1, bf16[32,256,256]{2,1,0:T(8,128)(2,1)} %constant.4.clone.high_hbm, bf16[32,256,256]{2,1,0:T(8,128)(2,1)} %constant.5.clone.low_hbm, f32[16,4096]{1,0:T(8,128)} %taps_ref.1, f32[4,128]{1,0:T(4,128)} %bitcast.1), custom_call_target="tpu_custom_call" | custom-call | tf_op jit(solution)/shard_map/correlator/pallas_call | solution.py:737
  170.5 1.6 copy.7

commit v7 on v6

--- a/solution.py
+++ b/solution.py
@@ -285,7 +285,7 @@
             work[1, k, spots, rows_of(g), :] = out[:, :, LANES:]
             return carry
 
-        lax.fori_loop(0, RADIX, second, 0, unroll=4)
+        lax.fori_loop(0, RADIX, second, 0, unroll=8)
 
     def await_prev(g):
         @pl.when(blk > 0)
@@ -395,9 +395,10 @@
             device_id=(c, blk), device_id_type=MESH,
         )
 
-    def sum_copy(r, sender):
-        return pltpu.make_async_remote_copy(
-            src_ref=sum_out.at[r], dst_ref=sum_in.at[sender], send_sem=sum_s.at[r], recv_sem=sum_r.at[sender],
+    def sum_copy(r, sender, j):
+        return pltpu.make_async_remote_copy(
+            src_ref=sum_out.at[r, j], dst_ref=sum_in.at[sender, j],
+            send_sem=sum_s.at[r, j], recv_sem=sum_r.at[sender, j],
             device_id=(stn, 2 * r + core), device_id_type=MESH,
         )
 
@@ -578,13 +579,13 @@
 
             def each(j, carry):
                 up(turn, r * quad + j, r, j)
+                if o > 0 and turn < ITERS - 1:
+                    sum_copy(r, place, j).start()
                 return carry
 
             lax.fori_loop(0, quad, each, 0)
             if turn == ITERS - 1:
                 send_half(r)
-            elif o > 0:
-                sum_copy(r, place).start()
 
         for o in sorted(range(places), key=lambda o: -min(o, places - o)):
             up_part(o)
@@ -600,7 +601,8 @@
         def await_sum(o, carry):
             r = peer_place(o)
             if turn < ITERS - 1:
-                sum_copy(r, r).wait_recv()
+                for m in range(quad):
+                    sum_copy(r, r, m).wait_recv()
             if turn > 0:
                 for m in range(quad):
                     weight_copy(r, place, m).wait_send()
@@ -653,7 +655,8 @@
             norm_copy(turn, c, stn).start()
 
         def sent(o, carry):
-            sum_copy(peer_place(o), place).wait_send()
+            for m in range(quad):
+                sum_copy(peer_place(o), place, m).wait_send()
             return carry
 
         lax.fori_loop(1, places, sent, 0)
@@ -782,8 +785,8 @@
             dma((stations,)),
             dma((stations,)),
             dma((stations,)),
-            dma((places,)),
-            dma((places,)),
+            dma((places, quad)),
+            dma((places, quad)),
             dma((places, quad)),
             dma((places, quad)),
             dma((ITERS - 1, stations)),

time: 172 us -> 169 us (0.983)
  Pallas kernels: 170 us -> 167 us
    pallas_call x1, Pallas kernels: 170 us -> 167 us  [correlate(): pl.pallas_call(functools.partial(correlator_kernel, stations, blocks), in...]
where the time goes in v7:
time: 169 us
  Pallas kernels  167 us (99%)
    pallas_call x1, Pallas kernels, correlate(): pl.pallas_call(functools.partial(correlator_kernel, stations, blocks), in...  167 us

profile of v7, /device:TPU:1, one launch (start us, length us, event | category | flops | bytes accessed | tf_op | source)
XLA Modules:
  0.0 168.8 jit_solution(7724669210482339258)
XLA Ops:
  0.0 167.2 %correlator.1 = f32[2,32,512]{2,1,0:T(8,128)} custom-call(bf16[2,32,65536]{2,1,0:T(8,128)(2,1)} %volt_ref.1, bf16[32,256,256]{2,1,0:T(8,128)(2,1)} %constant.4.clone.high_hbm, bf16[32,256,256]{2,1,0:T(8,128)(2,1)} %constant.5.clone.low_hbm, f32[16,4096]{1,0:T(8,128)} %taps_ref.1, f32[4,128]{1,0:T(4,128)} %bitcast.1), custom_call_target="tpu_custom_call" | custom-call | tf_op jit(solution)/shard_map/correlator/pallas_call | solution.py:740
  167.2 1.6 copy.7

commit v8 on v7

--- a/solution.py
+++ b/solution.py
@@ -285,7 +285,7 @@
             work[1, k, spots, rows_of(g), :] = out[:, :, LANES:]
             return carry
 
-        lax.fori_loop(0, RADIX, second, 0, unroll=8)
+        lax.fori_loop(0, RADIX, second, 0, unroll=16)
 
     def await_prev(g):
         @pl.when(blk > 0)

time: 169 us -> 169 us (level)
  no operation moved by 1% of the time
where the time goes in v8:
time: 169 us
  Pallas kernels  167 us (99%)
    pallas_call x1, Pallas kernels, correlate(): pl.pallas_call(functools.partial(correlator_kernel, stations, blocks), in...  167 us

profile of v8, /device:TPU:1, one launch (start us, length us, event | category | flops | bytes accessed | tf_op | source)
XLA Modules:
  0.0 168.6 jit_solution(3540264768367149502)
XLA Ops:
  0.0 167.0 %correlator.1 = f32[2,32,512]{2,1,0:T(8,128)} custom-call(bf16[2,32,65536]{2,1,0:T(8,128)(2,1)} %volt_ref.1, bf16[32,256,256]{2,1,0:T(8,128)(2,1)} %constant.4.clone.high_hbm, bf16[32,256,256]{2,1,0:T(8,128)(2,1)} %constant.5.clone.low_hbm, f32[16,4096]{1,0:T(8,128)} %taps_ref.1, f32[4,128]{1,0:T(4,128)} %bitcast.1), custom_call_target="tpu_custom_call" | custom-call | tf_op jit(solution)/shard_map/correlator/pallas_call | solution.py:740
  167.0 1.6 copy.7
